TPU v7x, 512 devices: a whole 4x8x8 slice. The times are simulated.
512 devices in a mesh: gy: 16 (over z, core), gx: 32 (over x, y).
Axes of the slice: x: 4, y: 8, z: 8, core: 2. Of those that a mesh axis runs over, the one named last changes fastest.
Arguments:
- points: bfloat16 [9, 2097152], P(None, ('gy', 'gx')), may hold values from -6 to 6
- point_pillar: int32 [2097152], P(('gy', 'gx')), may hold values from 0 to 4095, as said below
- point_weight: bfloat16 [9, 128], replicated, may hold values from -2 to 2
- recv_cell: int32 [2097152], P(('gy', 'gx')), may hold values from 0 to 511
- cell_mask: int32 [512, 512], P('gy', 'gx'), may hold values 0 or 1
- occupancy: int32 [512, 512], P('gy', 'gx'), may hold values 0 or 1
- conv_weight: bfloat16 [2, 9, 128, 128], replicated, may hold values from -0.1875 to 0.1875
- head_weight: bfloat16 [128], replicated, may hold values from -0.5 to 0.5
- conv_second: float32 [2, 9, 128, 128], replicated, may hold values from 1e-12 to 1e-07
- point_second: float32 [9, 128], replicated, may hold values from 1e-12 to 1e-07
- head_second: float32 [128], replicated, may hold values from 1e-10 to 1e-05
Outputs:
- conv_step: float32 [2, 9, 128, 128], replicated
- point_step: float32 [9, 128], replicated
- head_step: float32 [128], replicated
Inputs may be any that keep to these rules, and one draw needn't show every extreme that they name: `point_pillar`: on each device the ids do not fall; in each block of 128 slots the named slots are the first ones, every one named by at least one point, and on every device one block is full.
All inputs are finite; a program needn't handle non-finite values. No bound on the sum of `cell_mask` or of `occupancy` on one device may be relied on, other than what follows from the above.
Results may differ from a plain program's by a relative error of at most 0.009.
Values may be sent and summed in bfloat16 or wider, within the bound.
A program may use at most 64 MiB of HBM per device.

v0:
```python
import jax
import jax.numpy as jnp
from jax import lax
from jax.sharding import PartitionSpec as P


def with_halo(block, sides, width):
    for axis, dim in sides:
        count = lax.axis_size(axis)
        forward = [(i, i + 1) for i in range(count - 1)]
        backward = [(target, source) for source, target in forward]
        low = lax.ppermute(
            lax.slice_in_dim(block, block.shape[dim] - width, None, axis=dim), axis, forward
        )
        high = lax.ppermute(lax.slice_in_dim(block, 0, width, axis=dim), axis, backward)
        block = jnp.concatenate([low, block, high], axis=dim)
    return block


def silu_slope(value):
    sig = jax.nn.sigmoid(value)
    return sig * (1.0 + value * (1.0 - sig))


def stencil(padded, weights, out_rows, out_cols):
    channels = padded.shape[2]
    summed = jnp.zeros((out_rows * out_cols, weights.shape[2]), jnp.float32)
    for offset in range(9):
        shift_y, shift_x = divmod(offset, 3)
        window = padded[shift_y : shift_y + out_rows, shift_x : shift_x + out_cols].reshape(
            out_rows * out_cols, channels
        )
        summed = summed + jnp.dot(window, weights[offset], preferred_element_type=jnp.float32)
    return summed.reshape(out_rows, out_cols, weights.shape[2])


def kernel_grad(padded, grad_rows, out_rows, out_cols):
    channels = padded.shape[2]
    pieces = []
    for offset in range(9):
        shift_y, shift_x = divmod(offset, 3)
        window = padded[shift_y : shift_y + out_rows, shift_x : shift_x + out_cols].reshape(
            out_rows * out_cols, channels
        )
        pieces.append(jnp.dot(window.T, grad_rows, preferred_element_type=jnp.float32))
    return jnp.stack(pieces)


def rms_step(gradient, second):
    moment = 0.95 * second + 0.05 * gradient * gradient
    return gradient / (jnp.sqrt(moment) + 1e-08)


def grad_halo(gradient):
    return with_halo(gradient, (("gy", 0), ("gx", 1)), 1)


def on_device(
    points,
    point_pillar,
    point_weight,
    recv_cell,
    cell_mask,
    occupancy,
    conv_weight,
    head_weight,
    conv_second,
    point_second,
    head_second,
):
    columns = lax.axis_size("gx")
    tile_rows, tile_cols = cell_mask.shape
    rows_total = tile_rows * lax.axis_size("gy")
    cols_total = tile_cols * columns
    channels = point_weight.shape[1]
    slot_count = recv_cell.shape[0]
    block_size = slot_count // columns
    layers = conv_weight.shape[0]
    cell_count = tile_rows * tile_cols
    pre_points = jnp.einsum("fp,fc->pc", points, point_weight, preferred_element_type=jnp.float32)
    counts = jax.ops.segment_sum(
        jnp.ones(point_pillar.shape, jnp.float32),
        point_pillar,
        num_segments=slot_count,
        indices_are_sorted=True,
    )
    divisor = jnp.maximum(counts, 1.0)[:, None]
    pooled = jax.ops.segment_sum(
        jax.nn.silu(pre_points), point_pillar, num_segments=slot_count, indices_are_sorted=True
    )
    pillars = (pooled / divisor).astype(jnp.bfloat16)
    arrived = lax.all_to_all(
        pillars.reshape(columns, block_size, channels),
        "gx",
        split_axis=0,
        concat_axis=0,
        tiled=True,
    ).reshape(slot_count, channels)
    visible = (1 - cell_mask).astype(jnp.float32)
    placed = jax.ops.segment_sum(arrived.astype(jnp.float32), recv_cell, num_segments=cell_count)
    features = (placed.reshape(tile_rows, tile_cols, channels) * visible[:, :, None]).astype(
        jnp.bfloat16
    )
    padded_inputs = []
    pre_values = []
    current = features
    for layer_index in range(layers):
        padded = with_halo(current, (("gy", 0), ("gx", 1)), 1)
        padded_inputs.append(padded)
        pre_act = stencil(padded, conv_weight[layer_index], tile_rows, tile_cols)
        pre_values.append(pre_act)
        current = jax.nn.silu(pre_act).astype(jnp.bfloat16)
    logits = jnp.einsum("rcd,d->rc", current, head_weight, preferred_element_type=jnp.float32)
    masked = cell_mask.astype(jnp.float32)
    targets = occupancy.astype(jnp.float32)
    logit_grad = masked * (jax.nn.sigmoid(logits) - targets) / (rows_total * cols_total)
    head_local = jnp.einsum("rc,rcd->d", logit_grad, current.astype(jnp.float32))
    gradient = (
        logit_grad[:, :, None] * head_weight.astype(jnp.float32) * silu_slope(pre_values[-1])
    ).astype(jnp.bfloat16)
    kernel_terms = [None] * layers
    for layer_index in reversed(range(layers)):
        kernel_terms[layer_index] = kernel_grad(
            padded_inputs[layer_index], gradient.reshape(cell_count, channels), tile_rows, tile_cols
        )
        grad_padded = grad_halo(gradient)
        flipped = conv_weight[layer_index][::-1].transpose(0, 2, 1)
        backward = stencil(grad_padded, flipped, tile_rows, tile_cols)
        if layer_index > 0:
            gradient = (backward * silu_slope(pre_values[layer_index - 1])).astype(jnp.bfloat16)
        else:
            gradient = (backward * visible[:, :, None]).astype(jnp.bfloat16)
    pillar_grad = jnp.take(gradient.reshape(cell_count, channels), recv_cell, axis=0)
    returned = lax.all_to_all(
        pillar_grad.reshape(columns, block_size, channels),
        "gx",
        split_axis=0,
        concat_axis=0,
        tiled=True,
    ).reshape(slot_count, channels)
    slot_grad = returned.astype(jnp.float32) / divisor
    point_rows = (jnp.take(slot_grad, point_pillar, axis=0) * silu_slope(pre_points)).astype(
        jnp.bfloat16
    )
    point_local = jnp.einsum("fp,pc->fc", points, point_rows, preferred_element_type=jnp.float32)
    point_total, head_total = lax.psum((point_local, head_local), ("gy", "gx"))
    kernels = jnp.stack(kernel_terms)
    conv_total = lax.psum(kernels, ("gy", "gx"))
    conv_step = rms_step(conv_total, conv_second)
    return (conv_step, rms_step(point_total, point_second), rms_step(head_total, head_second))


def solution(mesh):
    return jax.shard_map(
        on_device,
        mesh=mesh,
        in_specs=(
            P(None, ("gy", "gx")),
            P(("gy", "gx")),
            P(),
            P(("gy", "gx")),
            P("gy", "gx"),
            P("gy", "gx"),
            P(),
            P(),
            P(),
            P(),
            P(),
        ),
        out_specs=(P(), P(), P()),
        check_vma=False,
    )
```

profile of v0, /device:TPU:1, one launch (start us, length us, event | category | flops | bytes accessed | tf_op | source)
XLA Modules:
  0.0 643.4 jit_solution(7597208051441638772)
XLA Ops:
  7.2 29.1 %scatter_custom_fusion.1 = f32[4096]{0:T(1024)S(1)} fusion(s32[4096]{0:T(1024)} %param.12, f32[4096]{0:T(1024)S(1)} %broadcast.55, f32[]{:T(128)} %constant.16.clone.1), kind=kCustom, calls=%fused_computation.213 | custom fusion | flops 4096 | bytes 16896 | tf_op jit(solution)/shard_map/scatter-add | solution.py:81
  36.3 2.5 fusion.110
  38.8 24.5 %scatter_custom_fusion = f32[4096,128]{1,0:T(8,128)S(1)} fusion(s32[4096]{0:T(1024)} %param.12, f32[4096,128]{1,0:T(8,128)} %fusion.110, f32[]{:T(128)} %constant.17.clone.1, f32[]{:T(128)} %constant.16.clone.1), kind=kCustom, calls=%fused_computation.10 | custom fusion | flops 2621440 | bytes 4195328 | tf_op jit(solution)/shard_map/scatter-add | solution.py:88
  63.3 1.5 divide_convert_fusion
  64.8 11.0 %all-to-all-start = ((bf16[32,128,128]{2,1,0:T(8,128)(2,1)}), bf16[32,128,128]{2,1,0:T(8,128)(2,1)S(1)}, u32[]{:S(2)}, u32[]{:S(2)}) async-start(bf16[32,128,128]{2,1,0:T(8,128)(2,1)} %bitcast), calls=%async_computation | async-start | bytes 2097152 | tf_op jit(solution)/shard_map/all_to_all | solution.py:92
  75.9 0.6 fusion.74
  76.5 24.1 %all-to-all-done = bf16[32,128,128]{2,1,0:T(8,128)(2,1)S(1)} async-done(((bf16[32,128,128]{2,1,0:T(8,128)(2,1)}), bf16[32,128,128]{2,1,0:T(8,128)(2,1)S(1)}, u32[]{:S(2)}, u32[]{:S(2)}) %all-to-all-start) | async-done | bytes 1048608 | tf_op jit(solution)/shard_map/all_to_all | solution.py:92
  100.6 22.5 %scatter_custom_fusion.2 = f32[512,128]{1,0:T(8,128)S(1)} fusion(s32[4096]{0:T(1024)S(1)} %copy-done.10, bf16[4096,128]{1,0:T(8,128)(2,1)S(1)} %bitcast.328, f32[]{:T(128)} %constant.16.clone.1), kind=kCustom, calls=%fused_computation.6 | custom fusion | flops 1048576 | bytes 1310724 | tf_op jit(solution)/shard_map/scatter-add | solution.py:100
  123.2 9.2 %collective-permute-start = (bf16[1,16,128]{2,0,1:T(2,128)(2,1)S(1)}, bf16[1,16,128]{2,0,1:T(2,128)(2,1)S(1)}, u32[]{:S(2)}, u32[]{:S(2)}) collective-permute-start(bf16[1,16,128]{2,0,1:T(2,128)(2,1)S(1)} %get-tuple-element.61), channel_id=1, source_target_pairs={{0,32},{32,64},{64,96},{96,128},{128,160},{160,192},{192,224},{224... | collective-permute-start | bytes 12296 | tf_op jit(solution)/shard_map/ppermute | solution.py:12
  132.5 1.9 collective-permute-start.1
  134.4 0.6 and_bitcast_fusion
  135.2 2.3 collective-permute-done.1
  137.4 1.3 collective-permute-start.3
  138.7 4.0 collective-permute-start.2
  143.0 0.6 collective-permute-done.2
  144.9 0.3 convolution_add_fusion.28
  146.0 3.1 collective-permute-start.4
  149.1 1.9 collective-permute-start.5
  151.1 0.8 reverse_bitcast_fusion
  151.9 2.2 collective-permute-done.5
  154.1 1.3 collective-permute-start.7
  155.4 4.5 collective-permute-start.6
  160.2 0.6 collective-permute-done.6
  163.2 0.3 fusion.82
  164.0 2.8 collective-permute-start.8
  166.8 2.1 collective-permute-start.9
  169.0 1.1 fusion.17
  170.3 0.2 fusion.15
  170.6 0.3 fusion.14
  170.9 0.2 fusion.13
  171.2 0.2 fusion.12
  171.4 0.2 fusion.11
  171.6 0.2 fusion.10
  171.9 1.3 collective-permute-start.11
  173.2 4.5 collective-permute-start.10
  178.0 0.6 collective-permute-done.10
  180.0 0.3 convolution_add_fusion.12
  181.3 0.9 fusion.27
  182.2 4.5 collective-permute-start.12
  186.7 1.9 collective-permute-start.13
  188.6 0.8 fusion.26
  189.5 0.9 fusion.25
  190.3 0.9 fusion.24
  191.2 0.5 collective-permute-done.13
  191.7 1.3 collective-permute-start.15
  193.0 4.5 collective-permute-start.14
  197.7 0.6 collective-permute-done.14
  200.7 12.1 %gather_fusion = bf16[4096,128]{1,0:T(8,128)(2,1)S(1)} fusion(bf16[512,128]{1,0:T(8,128)(2,1)S(1)} %fusion.9, s32[4096]{0:T(1024)S(1)} %copy-done.9), kind=kCustom, calls=%fused_computation | custom fusion | bytes 2113536 | tf_op jit(solution)/shard_map/jit(_take)/gather | solution.py:133
  212.9 1.5 broadcast_select_fusion
  214.4 13.2 %all-to-all-start.1 = ((bf16[32,128,128]{2,1,0:T(8,128)(2,1)}), bf16[32,128,128]{2,1,0:T(8,128)(2,1)S(1)}, u32[]{:S(2)}, u32[]{:S(2)}) async-start(bf16[32,128,128]{2,1,0:T(8,128)(2,1)} %broadcast_select_fusion), calls=%async_computation.1 | async-start | bytes 2097152 | tf_op jit(solution)/shard_map/all_to_all | solution.py:134
  227.7 1.0 fusion.23
  228.6 0.8 fusion.22
  229.5 0.9 fusion.21
  230.4 0.9 fusion.20
  231.2 0.9 fusion.19
  232.1 2.4 pad_maximum_fusion
  234.7 282.2 %all-reduce.3.cloned.1.call-done = f32[2,9,128,128]{3,2,1,0:T(8,128)} async-done(((f32[2,9,128,128]{3,2,1,0:T(8,128)}), f32[2,9,128,128]{3,2,1,0:T(8,128)}) %all-reduce.3.cloned.1.call-update) | async-done | bytes 1179664 | tf_op jit(solution)/shard_map/psum | solution.py:148
  517.0 2.8 fusion.7
  519.8 0.8 convert_divide_fusion
  520.6 14.2 %gather_fusion.1 = f32[4096,128]{1,0:T(8,128)} fusion(f32[4096,128]{1,0:T(8,128)S(1)} %convert_divide_fusion, s32[4096]{0:T(1024)S(1)} %fusion.73), kind=kCustom, calls=%fused_computation.1 | custom fusion | bytes 4210688 | tf_op jit(solution)/shard_map/jit(_take)/gather | solution.py:142
  534.8 4.3 convolution_bitcast_fusion.18
  539.1 96.3 %all-reduce = (f32[9,128]{1,0:T(8,128)S(1)}, f32[128]{0:T(128)S(1)}) all-reduce(f32[9,128]{1,0:T(8,128)S(1)} %convolution_bitcast_fusion.18, f32[128]{0:T(128)S(1)} %convolution_bitcast_fusion.19), channel_id=1, replica_groups=mesh['gy'=16,'gx'=32] {'gy','gx'}, use_global_device_ids=true, to_apply=%region_4.5 | all-reduce | flops 1280 | bytes 10240 | tf_op jit(solution)/shard_map/psum | solution.py:146
  635.4 0.6 fusion.78
  636.0 0.5 add_divide_fusion.5
  (167 shorter events, 11.4 us)
Async XLA Ops:
  7.2 29.1 %copy-start = (bf16[9,4096]{1,0:T(8,128)(2,1)S(1)}, bf16[9,4096]{1,0:T(8,128)(2,1)}, u32[]{:S(2)}) copy-start(bf16[9,4096]{1,0:T(8,128)(2,1)} %param.11) | copy-start | bytes 221188
  63.3 12.5 %copy-start.14 = (s32[32,16]{0,1:T(8,128)S(1)}, s32[32,16]{0,1:T(8,128)}, u32[]{:S(2)}) copy-start(s32[32,16]{0,1:T(8,128)} %param.15) | copy-start | bytes 6148
  63.3 12.6 %copy-start.10 = (s32[4096]{0:T(1024)S(1)}, s32[4096]{0:T(1024)}, u32[]{:S(2)}) copy-start(s32[4096]{0:T(1024)} %param.14) | copy-start | bytes 49156
  63.3 13.2 %copy-start.1 = (bf16[2,9,128,128]{3,2,1,0:T(8,128)(2,1)S(1)}, bf16[2,9,128,128]{3,2,1,0:T(8,128)(2,1)}, u32[]{:S(2)}) copy-start(bf16[2,9,128,128]{3,2,1,0:T(8,128)(2,1)} %param.17) | copy-start | bytes 1769476
  64.8 35.7 %all-to-all-start = ((bf16[32,128,128]{2,1,0:T(8,128)(2,1)}), bf16[32,128,128]{2,1,0:T(8,128)(2,1)S(1)}, u32[]{:S(2)}, u32[]{:S(2)}) async-start(bf16[32,128,128]{2,1,0:T(8,128)(2,1)} %bitcast), calls=%async_computation | async-start | bytes 2097152 | tf_op jit(solution)/shard_map/all_to_all | solution.py:92
  123.2 11.9 %collective-permute-start = (bf16[1,16,128]{2,0,1:T(2,128)(2,1)S(1)}, bf16[1,16,128]{2,0,1:T(2,128)(2,1)S(1)}, u32[]{:S(2)}, u32[]{:S(2)}) collective-permute-start(bf16[1,16,128]{2,0,1:T(2,128)(2,1)S(1)} %get-tuple-element.61), channel_id=1, source_target_pairs={{0,32},{32,64},{64,96},{96,128},{128,160},{160,192},{192,224},{224... | collective-permute-start | bytes 12296 | tf_op jit(solution)/shard_map/ppermute | solution.py:12
  132.5 5.0 collective-permute-start.1
  135.1 9.7 %copy-start.12 = (f32[512]{0:T(512)}, f32[512]{0:T(512)S(1)}, u32[]{:S(2)}) copy-start(f32[512]{0:T(512)S(1)} %mul.163) | copy-start | bytes 6148
  137.4 5.5 collective-permute-start.3
  138.7 4.8 collective-permute-start.2
  142.8 1.4 copy-start.6
  145.2 6.7 %copy-start.19 = (bf16[128]{0:T(256)(128)(2,1)S(1)}, bf16[128]{0:T(256)(128)(2,1)}, u32[]{:S(2)}) copy-start(bf16[128]{0:T(256)(128)(2,1)} %param.18) | copy-start | bytes 772
  146.0 5.9 collective-permute-start.4
  149.1 5.0 collective-permute-start.5
  151.9 18.7 %copy-start.20 = (f32[128]{0:T(128)}, f32[128]{0:T(128)S(1)}, u32[]{:S(2)}) copy-start(f32[128]{0:T(128)S(1)} %convert_element_type.77) | copy-start | bytes 1540
  154.1 6.1 collective-permute-start.7
  155.4 5.3 collective-permute-start.6
  160.1 1.3 copy-start.8
  162.1 1.3 copy-start.15
  162.1 1.3 copy-start.18
  164.0 7.8 %collective-permute-start.8 = (bf16[1,16,128]{2,0,1:T(2,128)(2,1)S(1)}, bf16[1,16,128]{2,0,1:T(2,128)(2,1)S(1)}, u32[]{:S(2)}, u32[]{:S(2)}) collective-permute-start(bf16[1,16,128]{2,0,1:T(2,128)(2,1)S(1)} %get-tuple-element.53), channel_id=1, source_target_pairs={{0,32},{32,64},{64,96},{96,128},{128,160},{160,192},{192,224},{224... | collective-permute-start | bytes 12296 | tf_op jit(solution)/shard_map/ppermute | solution.py:12
  166.8 5.1 collective-permute-start.9
  171.9 7.2 %copy-start.5 = (f32[9,128,128]{2,1,0:T(8,128)}, f32[9,128,128]{2,1,0:T(8,128)S(1)}, u32[]{:S(2)}) copy-start(f32[9,128,128]{2,1,0:T(8,128)S(1)} %fusion.10) | copy-start | bytes 1769476
  171.9 6.1 collective-permute-start.11
  173.2 5.3 collective-permute-start.10
  177.9 1.3 copy-start.4
  178.9 1.1 copy-start.21
  180.5 8.1 %copy-start.7 = (bf16[32,16,128]{2,0,1:T(8,128)(2,1)S(1)}, bf16[32,16,128]{2,0,1:T(8,128)(2,1)}, u32[]{:S(2)}) copy-start(bf16[32,16,128]{2,0,1:T(8,128)(2,1)} %copy-done.6) | copy-start | bytes 393220
  182.2 9.0 %collective-permute-start.12 = (bf16[1,16,128]{2,0,1:T(2,128)(2,1)S(1)}, bf16[1,16,128]{2,0,1:T(2,128)(2,1)S(1)}, u32[]{:S(2)}, u32[]{:S(2)}) collective-permute-start(bf16[1,16,128]{2,0,1:T(2,128)(2,1)S(1)} %get-tuple-element.49), channel_id=1, source_target_pairs={{0,32},{32,64},{64,96},{96,128},{128,160},{160,192},{192,224},{224... | collective-permute-start | bytes 12296 | tf_op jit(solution)/shard_map/ppermute | solution.py:12
  186.7 5.0 collective-permute-start.13
  191.7 6.1 collective-permute-start.15
  193.0 5.3 collective-permute-start.14
  197.6 1.3 copy-start.3
  199.3 1.2 copy-start.13
  199.5 1.2 copy-start.9
  200.7 12.2 %copy-start.16 = (pred[32,128]{1,0:T(8,128)(4,1)S(1)}, pred[32,128]{1,0:T(8,128)(4,1)}, u32[]{:S(2)}) copy-start(pred[32,128]{1,0:T(8,128)(4,1)} %and_bitcast_fusion) | copy-start | bytes 12292
  214.4 305.4 %all-to-all-start.1 = ((bf16[32,128,128]{2,1,0:T(8,128)(2,1)}), bf16[32,128,128]{2,1,0:T(8,128)(2,1)S(1)}, u32[]{:S(2)}, u32[]{:S(2)}) async-start(bf16[32,128,128]{2,1,0:T(8,128)(2,1)} %broadcast_select_fusion), calls=%async_computation.1 | async-start | bytes 2097152 | tf_op jit(solution)/shard_map/all_to_all | solution.py:134
  227.6 289.3 %all-reduce.3.cloned.1.call-start = ((), (), s32[]{:S(2)}) async-start(), calls=%async_computation.2 | async-start | bytes 2359296 | tf_op jit(solution)/shard_map/psum | solution.py:148
  231.2 3.3 copy-start.11
  231.2 285.7 %copy-start.2 = (f32[2,9,128,128]{3,2,1,0:T(8,128)S(1)}, f32[2,9,128,128]{3,2,1,0:T(8,128)}, u32[]{:S(2)}) copy-start(f32[2,9,128,128]{3,2,1,0:T(8,128)} %param.19) | copy-start | bytes 3538948
  534.8 100.6 %copy-start.17 = (f32[9,128]{1,0:T(8,128)S(1)}, f32[9,128]{1,0:T(8,128)}, u32[]{:S(2)}) copy-start(f32[9,128]{1,0:T(8,128)} %param.20) | copy-start | bytes 13828
  534.8 101.2 %copy-start.22 = (f32[128]{0:T(128)S(1)}, f32[128]{0:T(128)}, u32[]{:S(2)}) copy-start(f32[128]{0:T(128)} %param.21) | copy-start | bytes 1540
Sparse Core Ops, SparseCore 0:
  234.6 282.3 all-reduce.2
where the time goes:
time: 644 us; the launch traced here: 643 us
  waiting for transfers between devices  313 us (49%)
  blocking collectives  96.3 us (15%)
  other arithmetic  89 us (14%)
  starting transfers between devices  74.5 us (12%)
  local copies, waits for them, and re-layouts  30 us (5%)
  matrix products  24.8 us (4%)
  between operations  15.3 us (2%)
    psum x1, waiting for transfers between devices, on_device(): conv_total = lax.psum(kernels, ('gy', 'gx'))  282 us
    psum x1, blocking collectives, on_device(): point_total, head_total = lax.psum((point_local, head_local), ('gy', 'gx'))  96.3 us
    ppermute x8, starting transfers between devices, with_halo(): lax.ppermute(lax.slice_in_dim(block, block.shape[dim] - width, None, axis...  37.2 us
    scatter-add x1, other arithmetic, on_device(): jax.ops.segment_sum(jnp.ones(point_pillar.shape, jnp.float32), point_pill...  29.1 us
    scatter-add x1, other arithmetic, on_device(): jax.ops.segment_sum(jax.nn.silu(pre_points), point_pillar, num_segments=s...  24.5 us
    all_to_all x1, waiting for transfers between devices, on_device(): lax.all_to_all(pillars.reshape(columns, block_size, channels), 'gx', spli...  24.1 us
    scatter-add x1, other arithmetic, on_device(): jax.ops.segment_sum(arrived.astype(jnp.float32), recv_cell, num_segments=...  22.5 us
    gather x1, local copies, waits for them, and re-layouts, on_device(): jnp.take(slot_grad, point_pillar, axis=0) * silu_slope(pre_points)  14.2 us
  transfers between devices with their start and end apart: 19, of which 9 were waited for; matrix products, arithmetic and copies ran while one was open for 3% of the time, Pallas kernels for 0%

commit v1 on v0

v1 whole, which is shorter than its diff:
```python
import functools

import jax
import jax.numpy as jnp
from jax import lax
from jax.experimental import pallas as pl
from jax.experimental.pallas import tpu as pltpu
from jax.sharding import PartitionSpec as P

MESH = pl.DeviceIdType.MESH
F32 = jnp.float32
BF16 = jnp.bfloat16
VMEM_LIMIT = 56 * 1024 * 1024
CHUNK = 128
SIDE = 8
HALO = 4
STEPS = ((0, -1), (0, 1), (-1, 0), (1, 0), (-1, -1), (1, 1), (-1, 1), (1, -1))


def iota(shape, dim):
    return lax.broadcasted_iota(jnp.int32, shape, dim)


def dot(a, b):
    return jnp.dot(a, b, preferred_element_type=F32)


def dot_nt(a, b):
    return lax.dot_general(a, b, (((1,), (1,)), ((), ())), preferred_element_type=F32)


def dot_tn(a, b):
    return lax.dot_general(a, b, (((0,), (0,)), ((), ())), preferred_element_type=F32)


def slope(value):
    sig = jax.nn.sigmoid(value)
    return sig * (1.0 + value * (1.0 - sig))


def rms_step(gradient, second):
    moment = 0.95 * second + 0.05 * gradient * gradient
    return gradient / (jnp.sqrt(moment) + 1e-08)


def pool_kernel(
    points, ids, ids_row, weight, pillars, table, local, counts, table_s, partial, sums, numbers, sem
):
    chunks = ids.shape[0]
    blocks = pillars.shape[0] // CHUNK
    total = chunks * CHUNK
    here = ids[...]
    back = pltpu.roll(here, 1, axis=1)
    lane = iota(here.shape, 1)
    before = jnp.where(lane == 0, pltpu.roll(back, 1, axis=0), back)
    first = (lane == 0) & (iota(here.shape, 0) == 0)
    flags = jnp.where((here != before) | first, 1.0, 0.0).astype(BF16)
    upto = jnp.where(iota((CHUNK, CHUNK), 0) <= iota((CHUNK, CHUNK), 1), 1.0, 0.0).astype(BF16)
    inside = dot(flags, upto)
    whole = dot(flags, jnp.ones((CHUNK, CHUNK), BF16))
    lower = jnp.where(iota((chunks, chunks), 0) > iota((chunks, chunks), 1), 1.0, 0.0)
    ahead = dot(lower.astype(BF16), whole.astype(BF16))
    head = jnp.broadcast_to(inside[:, 0:1], inside.shape)
    local[...] = (inside - head).astype(jnp.int32)
    row = ids_row[...]
    row_before = pltpu.roll(row, 1, axis=1)
    row_first = (row != row_before) | (iota(row.shape, 1) == 0)
    row_block = jnp.where(row_first, row // CHUNK, blocks + 8)
    below = jnp.where(row_block < iota((blocks + 8, total), 0), 1.0, 0.0).astype(BF16)
    table[0:chunks, :] = (ahead + head - 1.0).astype(jnp.int32)
    table[chunks : chunks + blocks + 8, :] = dot(below, jnp.ones((total, CHUNK), BF16)).astype(
        jnp.int32
    )
    copy = pltpu.make_async_copy(table, table_s, sem)
    copy.start()
    ranks = local[...]
    for k in range(chunks):
        part = pl.ds(k * CHUNK, CHUNK)
        pre = dot_tn(points[:, part], weight[...])
        act = (pre * jax.nn.sigmoid(pre)).astype(BF16)
        pick = jnp.where(iota((CHUNK, CHUNK), 0) == ranks[k : k + 1, :], 1.0, 0.0).astype(BF16)
        partial[part, :] = dot(pick, jnp.concatenate([act, jnp.ones_like(act)], axis=1))
    copy.wait()
    edge = jnp.zeros((8, CHUNK), F32)
    for k in range(chunks):
        at = table_s[k, 0]
        for side, compact in enumerate((sums, numbers)):
            got = partial[pl.ds(k * CHUNK, CHUNK), pl.ds(side * CHUNK, CHUNK)]
            first_rows = got[0:8] if k == 0 else compact[pl.ds(at, 8), :] + got[0:8]
            compact[pl.ds(at, CHUNK + 8), :] = jnp.concatenate([first_rows, got[8:], edge], axis=0)
    diagonal = iota((CHUNK, CHUNK), 0) == iota((CHUNK, CHUNK), 1)
    for d in range(blocks):
        at = table_s[chunks + d, 0]
        held = table_s[chunks + d + 1, 0] - at
        named = iota((CHUNK, CHUNK), 0) < held
        count = jnp.where(named, numbers[pl.ds(at, CHUNK), :], 1.0)
        mean = jnp.where(named, sums[pl.ds(at, CHUNK), :] / count, 0.0)
        pillars[pl.ds(d * CHUNK, CHUNK), :] = mean.astype(BF16)
        counts[d : d + 1, :] = jnp.sum(jnp.where(diagonal, count, 0.0), axis=0, keepdims=True)


def pool(points, point_pillar, weight, slots):
    total = point_pillar.shape[0]
    chunks, blocks = total // CHUNK, slots // CHUNK
    channels = weight.shape[1]
    rows = chunks + blocks + 8
    vmem = pl.BlockSpec(memory_space=pltpu.VMEM)
    return pl.pallas_call(
        pool_kernel,
        out_shape=(
            jax.ShapeDtypeStruct((slots, channels), BF16),
            jax.ShapeDtypeStruct((rows, CHUNK), jnp.int32),
            jax.ShapeDtypeStruct((chunks, CHUNK), jnp.int32),
            jax.ShapeDtypeStruct((blocks, CHUNK), F32),
        ),
        in_specs=[vmem] * 4,
        out_specs=(vmem,) * 4,
        scratch_shapes=[
            pltpu.SMEM((rows, CHUNK), jnp.int32),
            pltpu.VMEM((total, 2 * CHUNK), F32),
            pltpu.VMEM((total + 2 * CHUNK, CHUNK), F32),
            pltpu.VMEM((total + 2 * CHUNK, CHUNK), F32),
            pltpu.SemaphoreType.DMA,
        ],
        compiler_params=pltpu.CompilerParams(vmem_limit_bytes=VMEM_LIMIT),
        name="pool",
    )(points, point_pillar.reshape(chunks, CHUNK), point_pillar.reshape(1, total), weight)


def point_kernel(points, local, weight, table_s, counts, returned, out, compact, rows):
    chunks = local.shape[0]
    blocks = counts.shape[0]
    pad = (-counts.shape[0]) % CHUNK
    scale = 1.0 / counts[...]
    scale = jnp.concatenate([scale, jnp.zeros((pad, CHUNK), F32)], axis=0).T
    for d in range(blocks):
        at = table_s[chunks + d, 0]
        block = returned[pl.ds(d * CHUNK, CHUNK), :].astype(F32)
        compact[pl.ds(at, CHUNK), :] = block * scale[:, d : d + 1]
    compact[pl.ds(table_s[chunks + blocks, 0], CHUNK), :] = jnp.zeros((CHUNK, CHUNK), F32)
    ranks = local[...].astype(F32)
    ranks = jnp.concatenate(
        [ranks, jnp.zeros(((-chunks) % CHUNK, CHUNK), F32)], axis=0
    ).T.astype(jnp.int32)
    for k in range(chunks):
        part = pl.ds(k * CHUNK, CHUNK)
        pre = dot_tn(points[:, part], weight[...])
        window = compact[pl.ds(table_s[k, 0], CHUNK), :].astype(BF16)
        pick = jnp.where(ranks[:, k : k + 1] == iota((CHUNK, CHUNK), 1), 1.0, 0.0).astype(BF16)
        rows[part, :] = (dot(pick, window) * slope(pre)).astype(BF16)
    out[...] = dot(points[...], rows[...])


def point_grad(points, local, weight, table, counts, returned):
    total = points.shape[1]
    vmem = pl.BlockSpec(memory_space=pltpu.VMEM)
    smem = pl.BlockSpec(memory_space=pltpu.SMEM)
    return pl.pallas_call(
        point_kernel,
        out_shape=jax.ShapeDtypeStruct(weight.shape, F32),
        in_specs=[vmem, vmem, vmem, smem, vmem, vmem],
        out_specs=vmem,
        scratch_shapes=[
            pltpu.VMEM((total + 2 * CHUNK, CHUNK), F32),
            pltpu.VMEM((total, CHUNK), BF16),
        ],
        compiler_params=pltpu.CompilerParams(vmem_limit_bytes=VMEM_LIMIT),
        name="point_grad",
    )(points, local, weight, table, counts, returned)


def message_rows(tile_rows, tile_cols):
    spans, at = [], 0
    for down, right in STEPS:
        size = (HALO if down else tile_rows) * (SIDE if right else tile_cols)
        spans.append((at, size))
        at += size
    return spans, at


def ring_size(columns):
    return {32: 8, 8: 4, 4: 2}[columns]


def ring_order(ring):
    order = [ring // 2]
    for far in range(ring // 2 - 1, 0, -1):
        order += [far, -far]
    return order + [0]


def map_kernel(
    grid,
    pillars,
    cells,
    mask_t,
    occupied_t,
    weights,
    head_row,
    returned,
    kernel_out,
    head_out,
    place,
    pick,
    send_f,
    got_f,
    send_m,
    got_m,
    v0,
    v1,
    v2,
    v3,
    send_i,
    got_i,
    got_x,
    send_y,
    got_y,
    own_g,
    got_g,
    send_r,
    own_k,
    core_k,
    send_k,
    got_kz,
    got_ky,
    got_kx,
    sem_f,
    sem_m,
    sem_i,
    sem_x,
    sem_y,
    sem_g,
    sem_r,
    sem_c,
    sem_kz,
    sem_ky,
    sem_kx,
):
    n_gy, n_gx, tile_rows, tile_cols = grid
    gy, gx = lax.axis_index("gy"), lax.axis_index("gx")
    ring = ring_size(n_gx)
    across = n_gx // ring
    half_ring = ring // 2
    order = ring_order(ring)
    slot_of = {rel: r for r, rel in enumerate(order)}
    slot_of[-half_ring] = slot_of[half_ring]
    x, y = gx // ring, lax.rem(gx, ring)
    channels = pillars.shape[1]
    spans, _ = message_rows(tile_rows, tile_cols)
    width = tile_cols + 2 * SIDE
    height = tile_rows + 2 * HALO
    count = tile_rows * tile_cols
    part_rows = count // 2
    fan = across * CHUNK

    def neighbour(k):
        down, right = STEPS[k]
        return lax.rem(gy + down + n_gy, n_gy), lax.rem(gx + right + n_gx, n_gx)

    def along(step):
        return lax.rem(y + step + ring, ring)

    def over(step):
        return lax.rem(x + step + across, across)

    def ring_device(step):
        return gy, x * ring + along(step)

    def across_device(step):
        return gy, over(step) * ring + y

    levels = n_gy // 2
    z, core = gy // 2, lax.rem(gy, 2)

    def level_device(step):
        return lax.rem(z + step, levels) * 2 + core, gx

    other_core = (z * 2 + 1 - core, gx)

    def slot_block(column, place_on_ring):
        return pl.ds(pl.multiple_of((column * ring + place_on_ring) * CHUNK, CHUNK), CHUNK)

    def remote(src, dst, send, recv, device):
        return pltpu.make_async_remote_copy(
            src_ref=src,
            dst_ref=dst,
            send_sem=send,
            recv_sem=recv,
            device_id=device,
            device_id_type=MESH,
        )

    def arrival(ref, sem):
        remote(ref, ref, sem, sem, ring_device(1)).wait_recv()

    barrier = pltpu.get_barrier_semaphore()
    partners = [neighbour(k) for k in range(len(STEPS))]
    partners += [ring_device(step) for step in range(1, ring)]
    partners += [across_device(step) for step in range(1, across)]
    partners += [level_device(step) for step in range(1, levels)] + [other_core]
    for device in partners:
        pl.semaphore_signal(barrier, inc=1, device_id=device, device_id_type=MESH)
    pl.semaphore_wait(barrier, len(partners))

    started = []

    def go(copy):
        copy.start()
        started.append(copy)

    def send_pillars(r):
        for o in range(1, across):
            go(
                remote(
                    pillars.at[slot_block(over(o), along(order[r]))],
                    got_x.at[pl.ds((r * across + o) * CHUNK, CHUNK)],
                    sem_x.at[0, r, o],
                    sem_x.at[1, r, o],
                    across_device(o),
                )
            )

    for r in range(min(3, ring)):
        send_pillars(r)

    send_i[...] = jnp.zeros_like(send_i)
    for step in range(ring):
        lead = step * 8
        for o in range(across):
            row = over(-o) * ring + along(step)
            send_i[lead + o : lead + o + 1, :] = cells[pl.ds(row, 1), :]
        if step == 0:
            got_i[pl.ds(slot_of[0] * 8, 8), :] = send_i[pl.ds(0, 8), :]
        else:
            rel = -step if step <= half_ring else ring - step
            slot = slot_of[rel]
            go(
                remote(
                    send_i.at[pl.ds(lead, 8)],
                    got_i.at[pl.ds(slot * 8, 8)],
                    sem_i.at[0, step],
                    sem_i.at[1, slot],
                    ring_device(step),
                )
            )

    def post(own, send, got, sem):
        grid3 = own.reshape(tile_rows, tile_cols, channels)
        for k, (down, right) in enumerate(STEPS):
            part = grid3
            if down:
                part = part[:HALO] if down < 0 else part[tile_rows - HALO :]
            if right:
                part = part[:, :SIDE] if right < 0 else part[:, tile_cols - SIDE :]
            at, size = spans[k]
            send[pl.ds(at, size), :] = part.reshape(size, channels).astype(BF16)
            there, _ = spans[k ^ 1]
            go(
                remote(
                    send.at[pl.ds(at, size)],
                    got.at[pl.ds(there, size)],
                    sem.at[0, k],
                    sem.at[1, k ^ 1],
                    neighbour(k),
                )
            )

    def collect(own, got, sem):
        parts = {}
        for k, (down, right) in enumerate(STEPS):
            at, size = spans[k]
            arrival(got.at[pl.ds(at, size)], sem.at[1, k])
            rows = HALO if down else tile_rows
            parts[down, right] = (
                got[pl.ds(at, size), :].astype(F32).reshape(rows, size // rows, channels)
            )
        parts[0, 0] = own.reshape(tile_rows, tile_cols, channels)
        return jnp.concatenate(
            [
                jnp.concatenate([parts[down, right] for right in (-1, 0, 1)], axis=1).reshape(
                    -1, channels
                )
                for down in (-1, 0, 1)
            ],
            axis=0,
        )

    masks = jnp.concatenate([mask_t[...], mask_t[...] * occupied_t[...]], axis=0)
    masks = masks.astype(F32).astype(BF16)
    of_row = iota((count, tile_rows), 0) // tile_cols == iota((count, tile_rows), 1)
    by_column = dot_nt(jnp.where(of_row, 1.0, 0.0).astype(BF16), masks)
    pairs = (count, 2 * tile_cols)
    of_column = iota(pairs, 0) % tile_cols == iota(pairs, 1) % tile_cols
    halves = (2 * tile_cols, channels)
    same_half = (iota(halves, 0) < tile_cols) == (iota(halves, 1) < channels // 2)
    mask_own = dot(
        jnp.where(of_column, by_column, 0.0).astype(BF16),
        jnp.where(same_half, 1.0, 0.0).astype(BF16),
    )
    post(mask_own, send_m, got_m, sem_m)

    flat = iota((height * width, channels), 0)
    row = flat // width + gy * tile_rows - HALO
    col = flat % width + gx * tile_cols - SIDE
    in_slab = jnp.where(
        (row >= 0) & (row < n_gy * tile_rows) & (col >= 0) & (col < n_gx * tile_cols), 1.0, 0.0
    )
    column = iota((tile_rows * width, channels), 0) % width
    own_column = jnp.where((column >= SIDE) & (column < SIDE + tile_cols), 1.0, 0.0)

    for r in range(ring - 1):
        arrival(got_i.at[pl.ds(r * 8, 8)], sem_i.at[1, r])
    rows_i = ring * 8
    cells_i = got_i[...]
    cells_t = jnp.concatenate(
        [cells_i.astype(F32), jnp.zeros(((-rows_i) % CHUNK, CHUNK), F32)], axis=0
    ).T.astype(jnp.int32)
    for r in range(ring):
        for o in range(across):
            at = r * 8 + o
            place[r, :, pl.ds(o * CHUNK, CHUNK)] = jnp.where(
                iota((count, CHUNK), 0) == cells_i[at : at + 1, :], 1.0, 0.0
            ).astype(BF16)
            pick[r, pl.ds(o * CHUNK, CHUNK), :] = jnp.where(
                cells_t[:, at : at + 1] == iota((CHUNK, count), 1), 1.0, 0.0
            ).astype(BF16)

    mask_all = (collect(mask_own, got_m, sem_m) * in_slab).astype(BF16)
    half = channels // 2
    spread = jnp.where(
        iota((channels, 2 * channels), 0)
        == jnp.where(iota((channels, 2 * channels), 1) < channels, 0, half),
        1.0,
        0.0,
    ).astype(BF16)
    mask_all = dot(mask_all, spread)
    hidden_cell = mask_all[:, :channels]
    target = mask_all[:, channels:]

    def cut(value, lead, rows):
        return value[lead * width : (lead + rows) * width]

    def side_by_side(value, ref):
        size = value.shape[0]
        left = pltpu.roll(value, 1, axis=0)
        right = pltpu.roll(value, size - 1, axis=0)
        ref[...] = jnp.concatenate([left.astype(BF16), value.astype(BF16), right.astype(BF16)], 1)

    def windows(ref, lead, rows):
        return jnp.concatenate(
            [ref[pl.ds((lead + a) * width, rows * width), :] for a in (0, 1, 2)], axis=1
        )

    def flipped(layer):
        return jnp.concatenate(
            [weights[layer, pl.ds((8 - k) * channels, channels), :] for k in range(9)], axis=1
        )

    visible = 1.0 - cut(hidden_cell, HALO, tile_rows).reshape(tile_rows, width, channels)[
        :, SIDE : SIDE + tile_cols
    ].reshape(count, channels)

    def placed_for(r):
        for o in range(1, across):
            arrival(got_x.at[pl.ds((r * across + o) * CHUNK, CHUNK)], sem_x.at[1, r, o])
        own = pillars[slot_block(x, along(order[r])), :]
        rest = got_x[pl.ds((r * across + 1) * CHUNK, fan - CHUNK), :]
        return dot(place[r], jnp.concatenate([own, rest], axis=0))

    sides = ((0, 1, pl.ds(0, part_rows)), (1, -1, pl.ds(part_rows, part_rows)))
    for t in range(half_ring):
        for r in range(2 * t + 1, min(2 * t + 3, ring)) if t else ():
            send_pillars(r)
        for side, step, part in sides:
            if t == 0:
                if side == 0:
                    summed = placed_for(0)
                    send_y[0, 0] = summed.astype(BF16)
                src = send_y.at[0, 0, part]
                dst = got_y.at[side, 0, part]
            else:
                summed = placed_for(slot_of[step * (half_ring - t)])
                before = got_y.at[side, t - 1]
                if t == 1:
                    arrival(before.at[part], sem_y.at[1, side, 0])
                    low, high = summed[:part_rows], summed[part_rows:]
                    if side == 0:
                        low = low + got_y[side, 0, part, :].astype(F32)
                    else:
                        high = high + got_y[side, 0, part, :].astype(F32)
                    summed = jnp.concatenate([low, high], axis=0)
                else:
                    arrival(before, sem_y.at[1, side, t - 1])
                    summed = summed + before[...].astype(F32)
                send_y[side, t] = summed.astype(BF16)
                src = send_y.at[side, t]
                dst = got_y.at[side, t]
            go(remote(src, dst, sem_y.at[0, side, t], sem_y.at[1, side, t], ring_device(step)))
    placed = placed_for(slot_of[0])
    last = half_ring - 1
    if last:
        for side, _, _ in sides:
            arrival(got_y.at[side, last], sem_y.at[1, side, last])
            placed = placed + got_y[side, last].astype(F32)
    else:
        for side, _, part in sides:
            arrival(got_y.at[side, 0, part], sem_y.at[1, side, 0])
        placed = placed + jnp.concatenate(
            [got_y[0, 0, pl.ds(0, part_rows), :], got_y[1, 0, pl.ds(part_rows, part_rows), :]], 0
        ).astype(F32)

    features = (placed * visible).astype(BF16).astype(F32)
    post(features, send_f, got_f, sem_f)
    side_by_side(collect(features, got_f, sem_f) * in_slab, v0)

    pre1 = dot(windows(v0, 0, height - 2), weights[0])
    side_by_side(pre1 * jax.nn.sigmoid(pre1) * cut(in_slab, 1, height - 2), v1)
    pre2 = dot(windows(v1, 0, height - 4), weights[1])
    sig2 = jax.nn.sigmoid(pre2)
    hidden2 = (pre2 * sig2).astype(BF16)
    head = jnp.broadcast_to(head_row[...], (channels, channels))
    logits = dot_nt(hidden2, head)
    cells_all = n_gy * tile_rows * n_gx * tile_cols
    logit_grad = (
        cut(hidden_cell, 2, height - 4) * jax.nn.sigmoid(logits) - cut(target, 2, height - 4)
    ) / cells_all
    grad2 = logit_grad * head_row[...].astype(F32) * (sig2 * (1.0 + pre2 * (1.0 - sig2)))
    side_by_side(grad2, v2)
    back2 = dot_nt(windows(v2, 0, height - 6), flipped(1))
    grad1 = back2 * slope(cut(pre1, 2, height - 6)) * cut(in_slab, 3, height - 6)
    side_by_side(grad1, v3)
    back1 = dot_nt(windows(v3, 0, tile_rows), flipped(0))
    back1 = back1.reshape(tile_rows, width, channels)[:, SIDE : SIDE + tile_cols].reshape(
        count, channels
    )
    own_g[...] = (back1 * visible).astype(BF16)

    def pass_on(t):
        for side, step, part in sides:
            src = own_g if t == 1 else got_g.at[side, t - 2]
            dst = got_g.at[side, t - 1]
            if t == half_ring:
                src, dst = src.at[part], dst.at[part]
            go(
                remote(
                    src, dst, sem_g.at[0, side, t - 1], sem_g.at[1, side, t - 1], ring_device(step)
                )
            )

    def hand_out(rel, gradient):
        r = slot_of[rel]
        rows = dot(pick[r], gradient).astype(BF16)
        returned[slot_block(x, along(rel)), :] = rows[:CHUNK]
        send_r[r] = rows
        for o in range(1, across):
            go(
                remote(
                    send_r.at[r, pl.ds(o * CHUNK, CHUNK)],
                    returned.at[slot_block(x, along(rel))],
                    sem_r.at[0, r, o],
                    sem_r.at[1, r, o],
                    across_device(-o),
                )
            )

    share = own_k.shape[2]

    def halve(layer, gradient):
        parts = levels // 2
        own_k[pl.ds(layer * parts, parts)] = gradient.reshape(
            parts, 2, share, channels
        ).astype(BF16)
        go(
            remote(
                own_k.at[pl.ds(layer * parts, parts), 1 - core],
                core_k.at[pl.ds(layer * parts, parts)],
                sem_c.at[0, layer],
                sem_c.at[1, layer],
                other_core,
            )
        )

    def to_levels():
        parts = levels // 2
        for layer in range(2):
            arrival(core_k.at[pl.ds(layer * parts, parts)], sem_c.at[1, layer])
        for k in range(levels):
            send_k[k] = (own_k[k, core].astype(F32) + core_k[k].astype(F32)).astype(BF16)
        got_kz[z] = send_k[z]
        for step in range(1, levels):
            go(
                remote(
                    send_k.at[lax.rem(z + step, levels)],
                    got_kz.at[z],
                    sem_kz.at[0, step],
                    sem_kz.at[1, step],
                    level_device(step),
                )
            )

    def gathered(got, sem):
        summed = None
        for step in range(1, got.shape[0]):
            arrival(got.at[0], sem.at[1, step])
        for k in range(got.shape[0]):
            term = got[k].astype(F32)
            summed = term if summed is None else summed + term
        return summed

    def to_all(summed, got, sem, me, device):
        got[me] = summed.astype(BF16)
        for step in range(1, got.shape[0]):
            go(remote(got.at[me], got.at[me], sem.at[0, step], sem.at[1, step], device(step)))

    pass_on(1)
    hand_out(0, own_g[...])
    own2 = (cut(grad2, 2, tile_rows) * own_column).astype(BF16)
    halve(1, dot_tn(windows(v1, 2, tile_rows), own2))
    for t in range(1, half_ring + 1):
        for side, _, part in sides:
            ref = got_g.at[side, t - 1]
            arrival(ref.at[part] if t == half_ring else ref, sem_g.at[1, side, t - 1])
        if t < half_ring:
            pass_on(t + 1)
            hand_out(-t, got_g[0, t - 1])
            hand_out(t, got_g[1, t - 1])
        else:
            hand_out(
                t,
                jnp.concatenate(
                    [
                        got_g[0, t - 1, pl.ds(0, part_rows), :],
                        got_g[1, t - 1, pl.ds(part_rows, part_rows), :],
                    ],
                    axis=0,
                ),
            )
        if t == 1:
            own1 = (cut(grad1, 1, tile_rows) * own_column).astype(BF16)
            halve(0, dot_tn(windows(v0, 3, tile_rows), own1))
            if half_ring == 1:
                to_levels()
        if t == 2:
            to_levels()
    to_all(gathered(got_kz, sem_kz), got_ky, sem_ky, y, ring_device)
    head_terms = cut(logit_grad * hidden2.astype(F32), 2, tile_rows) * own_column
    head_out[...] = jnp.sum(head_terms, axis=0, keepdims=True)
    to_all(gathered(got_ky, sem_ky), got_kx, sem_kx, x, across_device)
    for r, rel in enumerate(order):
        for o in range(1, across):
            arrival(returned.at[slot_block(over(o), along(rel))], sem_r.at[1, r, o])
    kernel_out[...] = gathered(got_kx, sem_kx)
    for copy in started:
        copy.wait_send()


def map_step(grid, pillars, recv_cell, cell_mask, occupancy, weights, head_weight):
    n_gy, n_gx, tile_rows, tile_cols = grid
    slots, channels = pillars.shape
    blocks = slots // CHUNK
    count = tile_rows * tile_cols
    width = tile_cols + 2 * SIDE
    height = tile_rows + 2 * HALO
    ring = ring_size(n_gx)
    across, half_ring = n_gx // ring, ring // 2
    _, rows = message_rows(tile_rows, tile_cols)
    vmem = pl.BlockSpec(memory_space=pltpu.VMEM)
    taps = weights.shape[1]
    levels = n_gy // 2
    share = 2 * taps * channels // n_gy
    return pl.pallas_call(
        functools.partial(map_kernel, grid),
        out_shape=(
            jax.ShapeDtypeStruct((slots, channels), BF16),
            jax.ShapeDtypeStruct((share, channels), F32),
            jax.ShapeDtypeStruct((1, channels), F32),
        ),
        in_specs=[vmem] * 6,
        out_specs=(vmem,) * 3,
        scratch_shapes=[
            pltpu.VMEM((ring, count, across * CHUNK), BF16),
            pltpu.VMEM((ring, across * CHUNK, count), BF16),
            pltpu.VMEM((rows, channels), BF16),
            pltpu.VMEM((rows, channels), BF16),
            pltpu.VMEM((rows, channels), BF16),
            pltpu.VMEM((rows, channels), BF16),
            pltpu.VMEM((height * width, 3 * channels), BF16),
            pltpu.VMEM(((height - 2) * width, 3 * channels), BF16),
            pltpu.VMEM(((height - 4) * width, 3 * channels), BF16),
            pltpu.VMEM(((height - 6) * width, 3 * channels), BF16),
            pltpu.VMEM((ring * 8, CHUNK), jnp.int32),
            pltpu.VMEM((ring * 8, CHUNK), jnp.int32),
            pltpu.VMEM((slots, channels), BF16),
            pltpu.VMEM((2, half_ring, count, channels), BF16),
            pltpu.VMEM((2, half_ring, count, channels), BF16),
            pltpu.VMEM((count, channels), BF16),
            pltpu.VMEM((2, half_ring, count, channels), BF16),
            pltpu.VMEM((ring, across * CHUNK, channels), BF16),
            pltpu.VMEM((levels, 2, share, channels), BF16),
            pltpu.VMEM((levels, share, channels), BF16),
            pltpu.VMEM((levels, share, channels), BF16),
            pltpu.VMEM((levels, share, channels), BF16),
            pltpu.VMEM((ring, share, channels), BF16),
            pltpu.VMEM((across, share, channels), BF16),
            pltpu.SemaphoreType.DMA((2, len(STEPS))),
            pltpu.SemaphoreType.DMA((2, len(STEPS))),
            pltpu.SemaphoreType.DMA((2, ring)),
            pltpu.SemaphoreType.DMA((2, ring, across)),
            pltpu.SemaphoreType.DMA((2, 2, half_ring)),
            pltpu.SemaphoreType.DMA((2, 2, half_ring)),
            pltpu.SemaphoreType.DMA((2, ring, across)),
            pltpu.SemaphoreType.DMA((2, 2)),
            pltpu.SemaphoreType.DMA((2, levels)),
            pltpu.SemaphoreType.DMA((2, ring)),
            pltpu.SemaphoreType.DMA((2, across)),
        ],
        compiler_params=pltpu.CompilerParams(
            vmem_limit_bytes=VMEM_LIMIT, collective_id=1, has_side_effects=True
        ),
        name="map_step",
    )(
        pillars,
        recv_cell.reshape(blocks, CHUNK),
        cell_mask.T,
        occupancy.T,
        weights.reshape(2, taps * channels, channels),
        head_weight.reshape(1, channels),
    )


def finish_kernel(
    grid,
    chunk,
    point_local,
    head_local,
    conv_second,
    point_second,
    head_second,
    conv_out,
    point_out,
    head_out,
    second,
    own_s,
    got_sz,
    got_sc,
    got_sy,
    got_sx,
    sem_l,
    sem_a,
    sem_p,
    sem_sz,
    sem_sc,
    sem_sy,
    sem_sx,
):
    n_gy, n_gx, _, _ = grid
    gy, gx = lax.axis_index("gy"), lax.axis_index("gx")
    ring = ring_size(n_gx)
    across = n_gx // ring
    levels = n_gy // 2
    x, y = gx // ring, lax.rem(gx, ring)
    z, core = gy // 2, lax.rem(gy, 2)
    share = chunk.shape[0]

    def level_device(step):
        return lax.rem(z + step, levels) * 2 + core, gx

    def ring_device(step):
        return gy, x * ring + lax.rem(y + step, ring)

    def across_device(step):
        return gy, lax.rem(x + step, across) * ring + y

    def core_device(step):
        return z * 2 + lax.rem(core + step, 2), gx

    def remote(src, dst, send, recv, device):
        return pltpu.make_async_remote_copy(
            src_ref=src,
            dst_ref=dst,
            send_sem=send,
            recv_sem=recv,
            device_id=device,
            device_id_type=MESH,
        )

    def arrival(ref, sem):
        remote(ref, ref, sem, sem, core_device(1)).wait_recv()

    load = pltpu.make_async_copy(
        conv_second.at[pl.ds(pl.multiple_of(gy * share, 8), share)], second, sem_l
    )
    load.start()
    barrier = pltpu.get_barrier_semaphore()
    partners = [ring_device(step) for step in range(1, ring)]
    partners += [across_device(step) for step in range(1, across)]
    partners += [level_device(step) for step in range(1, levels)] + [core_device(1)]
    for device in partners:
        pl.semaphore_signal(barrier, inc=1, device_id=device, device_id_type=MESH)
    pl.semaphore_wait(barrier, len(partners))

    started = []

    def go(copy):
        copy.start()
        started.append(copy)

    def to_all(value, got, sem, me, device):
        got[me] = value
        for step in range(1, got.shape[0]):
            go(remote(got.at[me], got.at[me], sem.at[0, step], sem.at[1, step], device(step)))

    def gathered(got, sem):
        for step in range(1, got.shape[0]):
            arrival(got.at[0], sem.at[1, step])
        summed = got[0]
        for k in range(1, got.shape[0]):
            summed = summed + got[k]
        return summed

    own_s[...] = jnp.zeros_like(own_s)
    own_s[0 : point_local.shape[0], :] = point_local[...]
    own_s[point_local.shape[0] : point_local.shape[0] + 1, :] = head_local[...]
    to_all(own_s[...], got_sy, sem_sy, y, ring_device)
    load.wait()
    conv_out[z * 2 + core] = rms_step(chunk[...], second[...]).astype(BF16)
    mine = conv_out.at[z * 2 + core]
    for step in range(1, levels):
        go(remote(mine, mine, sem_a.at[0, step], sem_a.at[1, step], level_device(step)))
    go(remote(mine, mine, sem_p.at[0, 0], sem_p.at[1, 0], core_device(1)))
    to_all(gathered(got_sy, sem_sy), got_sx, sem_sx, x, across_device)
    small = None
    for step in range(1, levels):
        level = lax.rem(z - step + levels, levels)
        held = conv_out.at[level * 2 + core]
        arrival(held, sem_a.at[1, step])
        go(remote(held, held, sem_p.at[0, step], sem_p.at[1, step], core_device(1)))
        if step == min(2, levels - 1):
            to_all(gathered(got_sx, sem_sx), got_sc, sem_sc, core, core_device)
        if step == min(4, levels - 1):
            to_all(gathered(got_sc, sem_sc), got_sz, sem_sz, z, level_device)
    small = gathered(got_sz, sem_sz)
    features = point_local.shape[0]
    point_out[...] = rms_step(small[:features], point_second[...])
    head_out[...] = rms_step(small[features : features + 1], head_second[...])
    for step in range(levels):
        level = lax.rem(z - step + levels, levels)
        arrival(conv_out.at[level * 2 + 1 - core], sem_p.at[1, step])
    for copy in started:
        copy.wait_send()


def finish(grid, chunk, point_local, head_local, conv_second, point_second, head_second):
    n_gy, n_gx, _, _ = grid
    share, channels = chunk.shape
    ring = ring_size(n_gx)
    across, levels = n_gx // ring, n_gy // 2
    rows = -(-(point_local.shape[0] + 1) // 8) * 8
    vmem = pl.BlockSpec(memory_space=pltpu.VMEM)
    return pl.pallas_call(
        functools.partial(finish_kernel, grid),
        out_shape=(
            jax.ShapeDtypeStruct((n_gy, share, channels), BF16),
            jax.ShapeDtypeStruct(point_local.shape, F32),
            jax.ShapeDtypeStruct((1, channels), F32),
        ),
        in_specs=[vmem, vmem, vmem, pl.BlockSpec(memory_space=pl.ANY), vmem, vmem],
        out_specs=(vmem,) * 3,
        scratch_shapes=[
            pltpu.VMEM((share, channels), F32),
            pltpu.VMEM((rows, channels), F32),
            pltpu.VMEM((levels, rows, channels), F32),
            pltpu.VMEM((2, rows, channels), F32),
            pltpu.VMEM((ring, rows, channels), F32),
            pltpu.VMEM((across, rows, channels), F32),
            pltpu.SemaphoreType.DMA,
            pltpu.SemaphoreType.DMA((2, levels)),
            pltpu.SemaphoreType.DMA((2, levels)),
            pltpu.SemaphoreType.DMA((2, levels)),
            pltpu.SemaphoreType.DMA((2, 2)),
            pltpu.SemaphoreType.DMA((2, ring)),
            pltpu.SemaphoreType.DMA((2, across)),
        ],
        compiler_params=pltpu.CompilerParams(
            vmem_limit_bytes=VMEM_LIMIT, collective_id=2, has_side_effects=True
        ),
        name="finish",
    )(
        chunk,
        point_local,
        head_local,
        conv_second.reshape(n_gy * share, channels),
        point_second,
        head_second.reshape(1, channels),
    )


def on_device(
    points,
    point_pillar,
    point_weight,
    recv_cell,
    cell_mask,
    occupancy,
    conv_weight,
    head_weight,
    conv_second,
    point_second,
    head_second,
):
    rows, columns = lax.axis_size("gy"), lax.axis_size("gx")
    tile_rows, tile_cols = cell_mask.shape
    channels = point_weight.shape[1]
    slots = recv_cell.shape[0]
    grid = (rows, columns, tile_rows, tile_cols)

    pillars, table, local, counts = pool(points, point_pillar, point_weight, slots)
    returned, kernels, head_local = map_step(
        grid, pillars, recv_cell, cell_mask, occupancy, conv_weight, head_weight
    )
    point_local = point_grad(points, local, point_weight, table, counts, returned)
    conv_step, point_step, head_step = finish(
        grid, kernels, point_local, head_local, conv_second, point_second, head_second
    )
    return conv_step.astype(F32).reshape(conv_second.shape), point_step, head_step[0]


def solution(mesh):
    return jax.shard_map(
        on_device,
        mesh=mesh,
        in_specs=(
            P(None, ("gy", "gx")),
            P(("gy", "gx")),
            P(),
            P(("gy", "gx")),
            P("gy", "gx"),
            P("gy", "gx"),
            P(),
            P(),
            P(),
            P(),
            P(),
        ),
        out_specs=(P(), P(), P()),
        check_vma=False,
    )
```

time: 644 us -> 127 us (0.20)
  waiting for transfers between devices: 313 us -> 0 us
  Pallas kernels: 0 us -> 123 us
  blocking collectives: 96.3 us -> 0 us
  other arithmetic: 89 us -> 2.2 us
  starting transfers between devices: 74.5 us -> 0 us
  local copies, waits for them, and re-layouts: 30 us -> 1.12 us
  matrix products: 24.8 us -> 0 us
  between operations: 15.3 us -> 0.67 us
    psum x1 -> x0, waiting for transfers between devices: 282 us -> none  [on_device(): conv_total = lax.psum(kernels, ('gy', 'gx'))]
    pallas_call x0 -> x4, Pallas kernels: none -> 123 us  [the longest x1 89.2 us: map_step(): pl.pallas_call(functools.partial(map_kernel, grid), out_shape=(jax.ShapeD...]
    psum x1 -> x0, blocking collectives: 96.3 us -> none  [on_device(): point_total, head_total = lax.psum((point_local, head_local), ('gy', 'gx'))]
    scatter-add x3 -> x0, other arithmetic: 76 us -> none  [the longest x1 29.1 us: on_device(): jax.ops.segment_sum(jnp.ones(point_pillar.shape, jnp.float32), point_pill...]
    ppermute x16 -> x0, starting transfers between devices: 50.2 us -> none  [the longest x8 37.2 us: with_halo(): lax.ppermute(lax.slice_in_dim(block, block.shape[dim] - width, None, axis...]
    gather x2 -> x0, local copies, waits for them, and re-layouts: 26.3 us -> none  [the longest x1 14.2 us: on_device(): jnp.take(slot_grad, point_pillar, axis=0) * silu_slope(pre_points)]
    dot_general x58 -> x0, matrix products: 24.8 us -> none  [the longest x18 10.9 us: kernel_grad(): jnp.dot(window.T, grad_rows, preferred_element_type=jnp.float32)]
    all_to_all x2 -> x0, starting transfers between devices: 24.2 us -> none  [the longest x1 13.2 us: on_device(): lax.all_to_all(pillar_grad.reshape(columns, block_size, channels), 'gx',...]
  transfers between devices with their start and end apart: 19 -> 0, of which waited for: 9 -> 0; matrix products, arithmetic and copies ran while one was open for 3% -> 0% of each run, Pallas kernels for 0% -> 0%
where the time goes in v1:
time: 127 us
  Pallas kernels  123 us (97%)
  other arithmetic  2.2 us (2%)
    pallas_call x1, Pallas kernels, map_step(): pl.pallas_call(functools.partial(map_kernel, grid), out_shape=(jax.ShapeD...  89.2 us
    pallas_call x1, Pallas kernels, finish(): pl.pallas_call(functools.partial(finish_kernel, grid), out_shape=(jax.Sha...  23.1 us
    pallas_call x1, Pallas kernels, pool(): pl.pallas_call(pool_kernel, out_shape=(jax.ShapeDtypeStruct((slots, chann...  6.28 us
    pallas_call x1, Pallas kernels, point_grad(): pl.pallas_call(point_kernel, out_shape=jax.ShapeDtypeStruct(weight.shape,...  4.22 us

profile of v1, /device:TPU:1, one launch (start us, length us, event | category | flops | bytes accessed | tf_op | source)
XLA Modules:
  0.0 126.8 jit_solution(14688921931594802586)
XLA Ops:
  0.6 6.3 %pool.1 = (bf16[4096,128]{1,0:T(8,128)(2,1)}, s32[72,128]{1,0:T(8,128)}, s32[32,128]{1,0:T(8,128)}, f32[32,128]{1,0:T(8,128)}) custom-call(bf16[9,4096]{1,0:T(8,128)(2,1)} %points.3, s32[32,128]{1,0:T(8,128)} %bitcast.15, s32[1,4096]{1,0:T(1,128)} %bitcast.16, bf16[9,128]{1,0:T(8,128)(2,1)} %weight.3), custom_call_target="tpu_custom_call" | custom-call | tf_op jit(solution)/shard_map/pool/pallas_call | solution.py:108
  6.9 89.2 %map_step.1 = (bf16[4096,128]{1,0:T(8,128)(2,1)}, f32[144,128]{1,0:T(8,128)}, f32[1,128]{1,0:T(1,128)}) custom-call(bf16[4096,128]{1,0:T(8,128)(2,1)} %get-tuple-element.13.pillars, s32[32,128]{1,0:T(8,128)} %bitcast.17, s32[16,32]{1,0:T(8,128)} %bitcast.18, s32[16,32]{1,0:T(8,128)} %bitcast.19, bf16[2,1152,128]{2,1,0:T(8,128)(2,1)} %bitcast.14, ...), custom_call_target="tpu_custom_call" | custom-call | tf_op jit(solution)/shard_map/map_step/pallas_call | solution.py:671
  96.2 4.2 %point_grad.1.point_local = f32[9,128]{1,0:T(8,128)} custom-call(bf16[9,4096]{1,0:T(8,128)(2,1)} %points.3, s32[32,128]{1,0:T(8,128)} %get-tuple-element.15.local, bf16[9,128]{1,0:T(8,128)(2,1)} %weight.3, s32[72,128]{1,0:T(8,128)} %get-tuple-element.16.table_s, f32[32,128]{1,0:T(8,128)} %get-tuple-element.17.counts, ...), custom_call_target="tpu_custom_call" | custom-call | tf_op jit(solution)/shard_map/point_grad/pallas_call | solution.py:158
  100.4 23.1 %finish.1 = (bf16[16,144,128]{2,1,0:T(8,128)(2,1)}, f32[9,128]{1,0:T(8,128)}, f32[1,128]{1,0:T(1,128)}) custom-call(f32[144,128]{1,0:T(8,128)} %get-tuple-element.14.chunk, f32[9,128]{1,0:T(8,128)} %point_grad.1.point_local, f32[1,128]{1,0:T(1,128)} %get-tuple-element.19.head_local, f32[2304,128]{1,0:T(8,128)} %bitcast.12, f32[9,128]{1,0:T(8,128)} %point_second.1, ...), custom_call_target="tpu_custom_call" | custom-call | tf_op jit(solution)/shard_map/finish/pallas_call | solution.py:860
  123.5 0.0 copy-start
  123.5 0.0 copy-start.1
  123.5 2.2 %convert.1 = f32[2,9,128,128]{3,2,1,0:T(8,128)} convert(bf16[2,9,128,128]{3,2,1,0:T(8,128)(2,1)} %bitcast.13) | non-fusion elementwise | flops 294912 | bytes 1769472 | tf_op jit(solution)/shard_map/reshape | solution.py:925
  125.7 0.0 copy-done
  125.7 0.6 copy.16
  126.3 0.0 copy-done.1
  126.3 0.5 copy.17
Async XLA Ops:
  123.5 2.2 %copy-start = (f32[9,128]{1,0:T(8,128)S(1)}, f32[9,128]{1,0:T(8,128)}, u32[]{:S(2)}) copy-start(f32[9,128]{1,0:T(8,128)} %get-tuple-element.27) | copy-start | bytes 13828
  123.5 2.8 %copy-start.1 = (f32[1,128]{1,0:T(1,128)S(1)}, f32[1,128]{1,0:T(1,128)}, u32[]{:S(2)}) copy-start(f32[1,128]{1,0:T(1,128)} %get-tuple-element.22) | copy-start | bytes 1540

commit v2 on v1

--- a/solution.py
+++ b/solution.py
@@ -127,48 +127,6 @@
     )(points, point_pillar.reshape(chunks, CHUNK), point_pillar.reshape(1, total), weight)
 
 
-def point_kernel(points, local, weight, table_s, counts, returned, out, compact, rows):
-    chunks = local.shape[0]
-    blocks = counts.shape[0]
-    pad = (-counts.shape[0]) % CHUNK
-    scale = 1.0 / counts[...]
-    scale = jnp.concatenate([scale, jnp.zeros((pad, CHUNK), F32)], axis=0).T
-    for d in range(blocks):
-        at = table_s[chunks + d, 0]
-        block = returned[pl.ds(d * CHUNK, CHUNK), :].astype(F32)
-        compact[pl.ds(at, CHUNK), :] = block * scale[:, d : d + 1]
-    compact[pl.ds(table_s[chunks + blocks, 0], CHUNK), :] = jnp.zeros((CHUNK, CHUNK), F32)
-    ranks = local[...].astype(F32)
-    ranks = jnp.concatenate(
-        [ranks, jnp.zeros(((-chunks) % CHUNK, CHUNK), F32)], axis=0
-    ).T.astype(jnp.int32)
-    for k in range(chunks):
-        part = pl.ds(k * CHUNK, CHUNK)
-        pre = dot_tn(points[:, part], weight[...])
-        window = compact[pl.ds(table_s[k, 0], CHUNK), :].astype(BF16)
-        pick = jnp.where(ranks[:, k : k + 1] == iota((CHUNK, CHUNK), 1), 1.0, 0.0).astype(BF16)
-        rows[part, :] = (dot(pick, window) * slope(pre)).astype(BF16)
-    out[...] = dot(points[...], rows[...])
-
-
-def point_grad(points, local, weight, table, counts, returned):
-    total = points.shape[1]
-    vmem = pl.BlockSpec(memory_space=pltpu.VMEM)
-    smem = pl.BlockSpec(memory_space=pltpu.SMEM)
-    return pl.pallas_call(
-        point_kernel,
-        out_shape=jax.ShapeDtypeStruct(weight.shape, F32),
-        in_specs=[vmem, vmem, vmem, smem, vmem, vmem],
-        out_specs=vmem,
-        scratch_shapes=[
-            pltpu.VMEM((total + 2 * CHUNK, CHUNK), F32),
-            pltpu.VMEM((total, CHUNK), BF16),
-        ],
-        compiler_params=pltpu.CompilerParams(vmem_limit_bytes=VMEM_LIMIT),
-        name="point_grad",
-    )(points, local, weight, table, counts, returned)
-
-
 def message_rows(tile_rows, tile_cols):
     spans, at = [], 0
     for down, right in STEPS:
@@ -197,8 +155,16 @@
     occupied_t,
     weights,
     head_row,
-    returned,
-    kernel_out,
+    points,
+    local,
+    point_weight,
+    table,
+    counts,
+    conv_second,
+    point_second,
+    head_second,
+    conv_out,
+    point_out,
     head_out,
     place,
     pick,
@@ -218,12 +184,25 @@
     own_g,
     got_g,
     send_r,
+    returned,
     own_k,
     core_k,
     send_k,
     got_kz,
+    send_kx,
+    got_kx,
     got_ky,
-    got_kx,
+    got_ax,
+    second,
+    merge_a,
+    merge_b,
+    slopes,
+    picks,
+    rows_b,
+    own_s,
+    got_sy,
+    got_sx,
+    got_sz,
     sem_f,
     sem_m,
     sem_i,
@@ -233,8 +212,15 @@
     sem_r,
     sem_c,
     sem_kz,
+    sem_kx,
     sem_ky,
-    sem_kx,
+    sem_ax,
+    sem_az,
+    sem_ac,
+    sem_sy,
+    sem_sx,
+    sem_sz,
+    sem_l,
 ):
     n_gy, n_gx, tile_rows, tile_cols = grid
     gy, gx = lax.axis_index("gy"), lax.axis_index("gx")
@@ -277,6 +263,9 @@
 
     other_core = (z * 2 + 1 - core, gx)
 
+    def stack_device(step):
+        return lax.rem(gy + step, n_gy), gx
+
     def slot_block(column, place_on_ring):
         return pl.ds(pl.multiple_of((column * ring + place_on_ring) * CHUNK, CHUNK), CHUNK)
 
@@ -293,11 +282,19 @@
     def arrival(ref, sem):
         remote(ref, ref, sem, sem, ring_device(1)).wait_recv()
 
+    share = own_k.shape[2]
+    piece = got_ky.shape[1]
+    load = pltpu.make_async_copy(
+        conv_second.at[pl.ds(pl.multiple_of(gy * share, 8), share)],
+        second.at[pl.ds(0, share)],
+        sem_l,
+    )
+    load.start()
     barrier = pltpu.get_barrier_semaphore()
     partners = [neighbour(k) for k in range(len(STEPS))]
     partners += [ring_device(step) for step in range(1, ring)]
     partners += [across_device(step) for step in range(1, across)]
-    partners += [level_device(step) for step in range(1, levels)] + [other_core]
+    partners += [stack_device(step) for step in range(1, n_gy)]
     for device in partners:
         pl.semaphore_signal(barrier, inc=1, device_id=device, device_id_type=MESH)
     pl.semaphore_wait(barrier, len(partners))
@@ -415,16 +412,95 @@
     cells_t = jnp.concatenate(
         [cells_i.astype(F32), jnp.zeros(((-rows_i) % CHUNK, CHUNK), F32)], axis=0
     ).T.astype(jnp.int32)
-    for r in range(ring):
+    def build_place(r):
         for o in range(across):
             at = r * 8 + o
             place[r, :, pl.ds(o * CHUNK, CHUNK)] = jnp.where(
                 iota((count, CHUNK), 0) == cells_i[at : at + 1, :], 1.0, 0.0
             ).astype(BF16)
+
+    def build_pick(r):
+        for o in range(across):
+            at = r * 8 + o
             pick[r, pl.ds(o * CHUNK, CHUNK), :] = jnp.where(
                 cells_t[:, at : at + 1] == iota((CHUNK, count), 1), 1.0, 0.0
             ).astype(BF16)
 
+    def cut(value, lead, rows):
+        return value[lead * width : (lead + rows) * width]
+
+    def side_by_side(value, ref):
+        size = value.shape[0]
+        left = pltpu.roll(value, 1, axis=0)
+        right = pltpu.roll(value, size - 1, axis=0)
+        ref[...] = jnp.concatenate([left.astype(BF16), value.astype(BF16), right.astype(BF16)], 1)
+
+    def windows(ref, lead, rows):
+        return jnp.concatenate(
+            [ref[pl.ds((lead + a) * width, rows * width), :] for a in (0, 1, 2)], axis=1
+        )
+
+    def flipped(layer):
+        return jnp.concatenate(
+            [weights[layer, pl.ds((8 - k) * channels, channels), :] for k in range(9)], axis=1
+        )
+
+    def placed_for(r):
+        for o in range(1, across):
+            arrival(got_x.at[pl.ds((r * across + o) * CHUNK, CHUNK)], sem_x.at[1, r, o])
+        own = pillars[slot_block(x, along(order[r])), :]
+        rest = got_x[pl.ds((r * across + 1) * CHUNK, fan - CHUNK), :]
+        return dot(place[r], jnp.concatenate([own, rest], axis=0))
+
+    halves = (pl.ds(0, part_rows), pl.ds(part_rows, part_rows))
+
+    def half_of(value, half):
+        return value[half * part_rows : (half + 1) * part_rows]
+
+    def grow(t, side, half, value):
+        if t > 1 or (t == 1 and half == side):
+            arrival(got_y.at[side, t - 1, halves[half]], sem_y.at[1, side, t - 1, half])
+            value = value + got_y[side, t - 1, halves[half], :].astype(F32)
+        send_y[side, t, halves[half], :] = value.astype(BF16)
+        go(
+            remote(
+                send_y.at[side, t, halves[half]],
+                got_y.at[side, t, halves[half]],
+                sem_y.at[0, side, t, half],
+                sem_y.at[1, side, t, half],
+                ring_device(1 - 2 * side),
+            )
+        )
+
+    left = list(range(ring))
+    for t in range(half_ring):
+        for r in range(2 * t + 1, min(2 * t + 3, ring)) if t else ():
+            send_pillars(r)
+        if t == 0:
+            build_place(0)
+            summed = placed_for(0)
+            for side in (0, 1):
+                grow(0, side, side, half_of(summed, side))
+        else:
+            summed = {}
+            for side in (0, 1):
+                r = slot_of[(1 - 2 * side) * (half_ring - t)]
+                build_place(r)
+                summed[side] = placed_for(r)
+                if t == 1:
+                    grow(t, side, 1 - side, half_of(summed[side], 1 - side))
+            for order_half in (0, 1):
+                for side in (0, 1):
+                    half = 1 - side if order_half == 0 else side
+                    if t > 1 or half == side:
+                        grow(t, side, half, half_of(summed[side], half))
+        for r in left[:2]:
+            build_pick(r)
+        left = left[2:]
+    build_place(slot_of[0])
+    placed = placed_for(slot_of[0])
+    for r in left:
+        build_pick(r)
     mask_all = (collect(mask_own, got_m, sem_m) * in_slab).astype(BF16)
     half = channels // 2
     spread = jnp.where(
@@ -437,78 +513,20 @@
     hidden_cell = mask_all[:, :channels]
     target = mask_all[:, channels:]
 
-    def cut(value, lead, rows):
-        return value[lead * width : (lead + rows) * width]
-
-    def side_by_side(value, ref):
-        size = value.shape[0]
-        left = pltpu.roll(value, 1, axis=0)
-        right = pltpu.roll(value, size - 1, axis=0)
-        ref[...] = jnp.concatenate([left.astype(BF16), value.astype(BF16), right.astype(BF16)], 1)
-
-    def windows(ref, lead, rows):
-        return jnp.concatenate(
-            [ref[pl.ds((lead + a) * width, rows * width), :] for a in (0, 1, 2)], axis=1
-        )
-
-    def flipped(layer):
-        return jnp.concatenate(
-            [weights[layer, pl.ds((8 - k) * channels, channels), :] for k in range(9)], axis=1
-        )
-
     visible = 1.0 - cut(hidden_cell, HALO, tile_rows).reshape(tile_rows, width, channels)[
         :, SIDE : SIDE + tile_cols
     ].reshape(count, channels)
 
-    def placed_for(r):
-        for o in range(1, across):
-            arrival(got_x.at[pl.ds((r * across + o) * CHUNK, CHUNK)], sem_x.at[1, r, o])
-        own = pillars[slot_block(x, along(order[r])), :]
-        rest = got_x[pl.ds((r * across + 1) * CHUNK, fan - CHUNK), :]
-        return dot(place[r], jnp.concatenate([own, rest], axis=0))
-
-    sides = ((0, 1, pl.ds(0, part_rows)), (1, -1, pl.ds(part_rows, part_rows)))
-    for t in range(half_ring):
-        for r in range(2 * t + 1, min(2 * t + 3, ring)) if t else ():
-            send_pillars(r)
-        for side, step, part in sides:
-            if t == 0:
-                if side == 0:
-                    summed = placed_for(0)
-                    send_y[0, 0] = summed.astype(BF16)
-                src = send_y.at[0, 0, part]
-                dst = got_y.at[side, 0, part]
-            else:
-                summed = placed_for(slot_of[step * (half_ring - t)])
-                before = got_y.at[side, t - 1]
-                if t == 1:
-                    arrival(before.at[part], sem_y.at[1, side, 0])
-                    low, high = summed[:part_rows], summed[part_rows:]
-                    if side == 0:
-                        low = low + got_y[side, 0, part, :].astype(F32)
-                    else:
-                        high = high + got_y[side, 0, part, :].astype(F32)
-                    summed = jnp.concatenate([low, high], axis=0)
-                else:
-                    arrival(before, sem_y.at[1, side, t - 1])
-                    summed = summed + before[...].astype(F32)
-                send_y[side, t] = summed.astype(BF16)
-                src = send_y.at[side, t]
-                dst = got_y.at[side, t]
-            go(remote(src, dst, sem_y.at[0, side, t], sem_y.at[1, side, t], ring_device(step)))
-    placed = placed_for(slot_of[0])
     last = half_ring - 1
-    if last:
-        for side, _, _ in sides:
-            arrival(got_y.at[side, last], sem_y.at[1, side, last])
-            placed = placed + got_y[side, last].astype(F32)
-    else:
-        for side, _, part in sides:
-            arrival(got_y.at[side, 0, part], sem_y.at[1, side, 0])
-        placed = placed + jnp.concatenate(
-            [got_y[0, 0, pl.ds(0, part_rows), :], got_y[1, 0, pl.ds(part_rows, part_rows), :]], 0
-        ).astype(F32)
-
+    ends = []
+    for half in (0, 1):
+        value = half_of(placed, half)
+        for side in (0, 1):
+            if last or half == side:
+                arrival(got_y.at[side, last, halves[half]], sem_y.at[1, side, last, half])
+                value = value + got_y[side, last, halves[half], :].astype(F32)
+        ends.append(value)
+    placed = jnp.concatenate(ends, axis=0)
     features = (placed * visible).astype(BF16).astype(F32)
     post(features, send_f, got_f, sem_f)
     side_by_side(collect(features, got_f, sem_f) * in_slab, v0)
@@ -535,17 +553,17 @@
     )
     own_g[...] = (back1 * visible).astype(BF16)
 
-    def pass_on(t):
-        for side, step, part in sides:
-            src = own_g if t == 1 else got_g.at[side, t - 2]
-            dst = got_g.at[side, t - 1]
-            if t == half_ring:
-                src, dst = src.at[part], dst.at[part]
-            go(
-                remote(
-                    src, dst, sem_g.at[0, side, t - 1], sem_g.at[1, side, t - 1], ring_device(step)
-                )
-            )
+    def pass_on(t, side, half):
+        src = own_g if t == 1 else got_g.at[side, t - 2]
+        go(
+            remote(
+                src.at[halves[half]],
+                got_g.at[side, t - 1, halves[half]],
+                sem_g.at[0, side, t - 1, half],
+                sem_g.at[1, side, t - 1, half],
+                ring_device(1 - 2 * side),
+            )
+        )
 
     def hand_out(rel, gradient):
         r = slot_of[rel]
@@ -563,10 +581,9 @@
                 )
             )
 
-    share = own_k.shape[2]
+    parts = levels // 2
 
     def halve(layer, gradient):
-        parts = levels // 2
         own_k[pl.ds(layer * parts, parts)] = gradient.reshape(
             parts, 2, share, channels
         ).astype(BF16)
@@ -581,8 +598,7 @@
         )
 
     def to_levels():
-        parts = levels // 2
-        for layer in range(2):
+        for layer in (0, 1):
             arrival(core_k.at[pl.ds(layer * parts, parts)], sem_c.at[1, layer])
         for k in range(levels):
             send_k[k] = (own_k[k, core].astype(F32) + core_k[k].astype(F32)).astype(BF16)
@@ -607,56 +623,178 @@
             summed = term if summed is None else summed + term
         return summed
 
-    def to_all(summed, got, sem, me, device):
-        got[me] = summed.astype(BF16)
+    def to_all(value, got, sem, me, device):
+        got[me] = value.astype(got.dtype)
         for step in range(1, got.shape[0]):
             go(remote(got.at[me], got.at[me], sem.at[0, step], sem.at[1, step], device(step)))
 
-    pass_on(1)
-    hand_out(0, own_g[...])
+    def to_pieces(summed):
+        spare = across * piece - share
+        if spare:
+            summed = jnp.concatenate([summed, jnp.zeros((spare, channels), F32)], axis=0)
+        send_kx[...] = summed.reshape(across, piece, channels).astype(BF16)
+        got_kx[x] = send_kx[x]
+        for step in range(1, across):
+            go(
+                remote(
+                    send_kx.at[over(step)],
+                    got_kx.at[x],
+                    sem_kx.at[0, step],
+                    sem_kx.at[1, step],
+                    across_device(step),
+                )
+            )
+
+    def take_step(summed):
+        load.wait()
+        if across * piece > share:
+            second[pl.ds(share, across * piece - share), :] = jnp.ones(
+                (across * piece - share, channels), F32
+            )
+        rows = pl.ds(pl.multiple_of(x * piece, 8), piece)
+        return rms_step(summed, second[rows, :])
+
+    chunks = local.shape[0]
+    blocks = counts.shape[0]
+
+    def turned(value):
+        spare = (-value.shape[0]) % CHUNK
+        return jnp.concatenate([value, jnp.zeros((spare, CHUNK), F32)], axis=0).T
+
+    ranks_t = turned(local[...].astype(F32)).astype(jnp.int32)
+
+    def prepare(begin, end):
+        for k in range(begin, end):
+            part = pl.ds(k * CHUNK, CHUNK)
+            slopes[part, :] = slope(dot_tn(points[:, part], point_weight[...]))
+            picks[part, :] = jnp.where(
+                ranks_t[:, k : k + 1] == iota((CHUNK, CHUNK), 1), 1.0, 0.0
+            ).astype(BF16)
+
+    scale = turned(1.0 / counts[...])
+
+    def start_merge():
+        for d in range(blocks):
+            part = pl.ds(d * CHUNK, CHUNK)
+            merge_a[part, :] = returned[part, :].astype(F32) * scale[:, d : d + 1]
+        spare = merge_a.shape[0] - blocks * CHUNK
+        for ref in (merge_a, merge_b):
+            ref[pl.ds(blocks * CHUNK, spare), :] = jnp.zeros((spare, CHUNK), F32)
+
+    def merge_level(level, src, dst):
+        size = CHUNK << level
+        for pair in range(blocks >> (level + 1)):
+            lead = pair * 2 * size
+            first = chunks + pair * (2 << level)
+            held = table[first + (1 << level), 0] - table[first, 0]
+            for at in range(0, 2 * size, 2 * CHUNK):
+                rows = iota((2 * CHUNK, CHUNK), 0) + at
+                dst[pl.ds(lead + at, 2 * CHUNK), :] = jnp.where(
+                    rows < held,
+                    src[pl.ds(lead + at, 2 * CHUNK), :],
+                    src[pl.ds(lead + at + size - held, 2 * CHUNK), :],
+                )
+
+    levels_m = blocks.bit_length() - 1
+    refs = (merge_a, merge_b)
+
+    def merge(begin, end):
+        for level in range(begin, end):
+            merge_level(level, refs[level % 2], refs[1 - level % 2])
+
+    def point_terms():
+        joined = refs[levels_m % 2]
+        for k in range(chunks):
+            part = pl.ds(k * CHUNK, CHUNK)
+            window = joined[pl.ds(table[k, 0], CHUNK), :].astype(BF16)
+            rows_b[part, :] = (dot(picks[part, :], window) * slopes[part, :]).astype(BF16)
+        return dot(points[...], rows_b[...])
+
+    for order_half in (0, 1):
+        for side in (0, 1):
+            pass_on(1, side, side if order_half == 0 else 1 - side)
+    own1 = (cut(grad1, 1, tile_rows) * own_column).astype(BF16)
+    halve(0, dot_tn(windows(v0, 3, tile_rows), own1))
     own2 = (cut(grad2, 2, tile_rows) * own_column).astype(BF16)
     halve(1, dot_tn(windows(v1, 2, tile_rows), own2))
+    hand_out(0, own_g[...])
+    head_terms = cut(logit_grad * hidden2.astype(F32), 2, tile_rows) * own_column
+    head_local = jnp.sum(head_terms, axis=0, keepdims=True)
+    prepared = 0
     for t in range(1, half_ring + 1):
-        for side, _, part in sides:
-            ref = got_g.at[side, t - 1]
-            arrival(ref.at[part] if t == half_ring else ref, sem_g.at[1, side, t - 1])
         if t < half_ring:
-            pass_on(t + 1)
-            hand_out(-t, got_g[0, t - 1])
-            hand_out(t, got_g[1, t - 1])
+            for order_half in (0, 1):
+                for side in (0, 1):
+                    half = side if order_half == 0 else 1 - side
+                    arrival(got_g.at[side, t - 1, halves[half]], sem_g.at[1, side, t - 1, half])
+                    if t + 1 < half_ring or order_half == 0:
+                        pass_on(t + 1, side, half)
         else:
+            for side in (0, 1):
+                arrival(got_g.at[side, t - 1, halves[side]], sem_g.at[1, side, t - 1, side])
+        if t == 1:
+            to_levels()
+        if t == half_ring:
+            to_pieces(gathered(got_kz, sem_kz))
             hand_out(
                 t,
                 jnp.concatenate(
-                    [
-                        got_g[0, t - 1, pl.ds(0, part_rows), :],
-                        got_g[1, t - 1, pl.ds(part_rows, part_rows), :],
-                    ],
-                    axis=0,
+                    [got_g[side, t - 1, halves[side], :] for side in (0, 1)], axis=0
                 ),
             )
-        if t == 1:
-            own1 = (cut(grad1, 1, tile_rows) * own_column).astype(BF16)
-            halve(0, dot_tn(windows(v0, 3, tile_rows), own1))
-            if half_ring == 1:
-                to_levels()
-        if t == 2:
-            to_levels()
-    to_all(gathered(got_kz, sem_kz), got_ky, sem_ky, y, ring_device)
-    head_terms = cut(logit_grad * hidden2.astype(F32), 2, tile_rows) * own_column
-    head_out[...] = jnp.sum(head_terms, axis=0, keepdims=True)
-    to_all(gathered(got_ky, sem_ky), got_kx, sem_kx, x, across_device)
+        else:
+            hand_out(-t, got_g[0, t - 1])
+            hand_out(t, got_g[1, t - 1])
+        share_to = chunks * t // half_ring
+        prepare(prepared, share_to)
+        prepared = share_to
+    to_all(gathered(got_kx, sem_kx), got_ky, sem_ky, y, ring_device)
     for r, rel in enumerate(order):
         for o in range(1, across):
             arrival(returned.at[slot_block(over(o), along(rel))], sem_r.at[1, r, o])
-    kernel_out[...] = gathered(got_kx, sem_kx)
+    start_merge()
+    merge(0, min(2, levels_m))
+    to_all(take_step(gathered(got_ky, sem_ky)), got_ax, sem_ax, x, across_device)
+    merge(min(2, levels_m), levels_m)
+    for step in range(1, across):
+        arrival(got_ax.at[0], sem_ax.at[1, step])
+    conv_out[gy] = got_ax[...].reshape(across * piece, channels)[:share]
+    mine = conv_out.at[gy]
+    for step in range(1, levels):
+        go(remote(mine, mine, sem_az.at[0, step], sem_az.at[1, step], level_device(step)))
+    go(remote(mine, mine, sem_ac.at[0, 0], sem_ac.at[1, 0], other_core))
+    features_in = points.shape[0]
+    own_s[...] = jnp.zeros_like(own_s)
+    own_s[0:features_in, :] = point_terms()
+    own_s[features_in : features_in + 1, :] = head_local
+    to_all(own_s[...], got_sy, sem_sy, y, ring_device)
+
+    def relay(begin, end):
+        for step in range(begin, end):
+            held = conv_out.at[lax.rem(z - step + levels, levels) * 2 + core]
+            arrival(held, sem_az.at[1, step])
+            go(remote(held, held, sem_ac.at[0, step], sem_ac.at[1, step], other_core))
+
+    relay(1, min(3, levels))
+    to_all(gathered(got_sy, sem_sy), got_sx, sem_sx, x, across_device)
+    relay(min(3, levels), min(6, levels))
+    to_all(gathered(got_sx, sem_sx), got_sz, sem_sz, gy, stack_device)
+    relay(min(6, levels), levels)
+    small = gathered(got_sz, sem_sz)
+    point_out[...] = rms_step(small[:features_in], point_second[...])
+    head_out[...] = rms_step(small[features_in : features_in + 1], head_second[...])
+    for step in range(levels):
+        level = lax.rem(z - step + levels, levels)
+        arrival(conv_out.at[level * 2 + 1 - core], sem_ac.at[1, step])
     for copy in started:
         copy.wait_send()
 
 
-def map_step(grid, pillars, recv_cell, cell_mask, occupancy, weights, head_weight):
+def map_step(grid, pillars, recv_cell, cell_mask, occupancy, weights, head_weight, points, local,
+             point_weight, table, counts, conv_second, point_second, head_second):
     n_gy, n_gx, tile_rows, tile_cols = grid
     slots, channels = pillars.shape
+    total = points.shape[1]
     blocks = slots // CHUNK
     count = tile_rows * tile_cols
     width = tile_cols + 2 * SIDE
@@ -665,17 +803,20 @@
     across, half_ring = n_gx // ring, ring // 2
     _, rows = message_rows(tile_rows, tile_cols)
     vmem = pl.BlockSpec(memory_space=pltpu.VMEM)
+    smem = pl.BlockSpec(memory_space=pltpu.SMEM)
     taps = weights.shape[1]
     levels = n_gy // 2
     share = 2 * taps * channels // n_gy
+    piece = -(-share // (across * 16)) * 16
+    few = -(-(points.shape[0] + 1) // 8) * 8
     return pl.pallas_call(
         functools.partial(map_kernel, grid),
         out_shape=(
-            jax.ShapeDtypeStruct((slots, channels), BF16),
-            jax.ShapeDtypeStruct((share, channels), F32),
+            jax.ShapeDtypeStruct((n_gy, share, channels), BF16),
+            jax.ShapeDtypeStruct(point_weight.shape, F32),
             jax.ShapeDtypeStruct((1, channels), F32),
         ),
-        in_specs=[vmem] * 6,
+        in_specs=[vmem] * 9 + [smem, vmem, pl.BlockSpec(memory_space=pl.ANY), vmem, vmem],
         out_specs=(vmem,) * 3,
         scratch_shapes=[
             pltpu.VMEM((ring, count, across * CHUNK), BF16),
@@ -696,23 +837,43 @@
             pltpu.VMEM((count, channels), BF16),
             pltpu.VMEM((2, half_ring, count, channels), BF16),
             pltpu.VMEM((ring, across * CHUNK, channels), BF16),
+            pltpu.VMEM((slots, channels), BF16),
             pltpu.VMEM((levels, 2, share, channels), BF16),
             pltpu.VMEM((levels, share, channels), BF16),
             pltpu.VMEM((levels, share, channels), BF16),
             pltpu.VMEM((levels, share, channels), BF16),
-            pltpu.VMEM((ring, share, channels), BF16),
-            pltpu.VMEM((across, share, channels), BF16),
+            pltpu.VMEM((across, piece, channels), BF16),
+            pltpu.VMEM((across, piece, channels), BF16),
+            pltpu.VMEM((ring, piece, channels), BF16),
+            pltpu.VMEM((across, piece, channels), BF16),
+            pltpu.VMEM((across * piece, channels), F32),
+            pltpu.VMEM((slots + slots // 2, channels), F32),
+            pltpu.VMEM((slots + slots // 2, channels), F32),
+            pltpu.VMEM((total, channels), F32),
+            pltpu.VMEM((total, CHUNK), BF16),
+            pltpu.VMEM((total, channels), BF16),
+            pltpu.VMEM((few, channels), F32),
+            pltpu.VMEM((ring, few, channels), F32),
+            pltpu.VMEM((across, few, channels), F32),
+            pltpu.VMEM((n_gy, few, channels), F32),
             pltpu.SemaphoreType.DMA((2, len(STEPS))),
             pltpu.SemaphoreType.DMA((2, len(STEPS))),
             pltpu.SemaphoreType.DMA((2, ring)),
             pltpu.SemaphoreType.DMA((2, ring, across)),
-            pltpu.SemaphoreType.DMA((2, 2, half_ring)),
-            pltpu.SemaphoreType.DMA((2, 2, half_ring)),
+            pltpu.SemaphoreType.DMA((2, 2, half_ring, 2)),
+            pltpu.SemaphoreType.DMA((2, 2, half_ring, 2)),
             pltpu.SemaphoreType.DMA((2, ring, across)),
             pltpu.SemaphoreType.DMA((2, 2)),
             pltpu.SemaphoreType.DMA((2, levels)),
+            pltpu.SemaphoreType.DMA((2, across)),
             pltpu.SemaphoreType.DMA((2, ring)),
             pltpu.SemaphoreType.DMA((2, across)),
+            pltpu.SemaphoreType.DMA((2, levels)),
+            pltpu.SemaphoreType.DMA((2, levels)),
+            pltpu.SemaphoreType.DMA((2, ring)),
+            pltpu.SemaphoreType.DMA((2, across)),
+            pltpu.SemaphoreType.DMA((2, n_gy)),
+            pltpu.SemaphoreType.DMA,
         ],
         compiler_params=pltpu.CompilerParams(
             vmem_limit_bytes=VMEM_LIMIT, collective_id=1, has_side_effects=True
@@ -725,170 +886,11 @@
         occupancy.T,
         weights.reshape(2, taps * channels, channels),
         head_weight.reshape(1, channels),
-    )
-
-
-def finish_kernel(
-    grid,
-    chunk,
-    point_local,
-    head_local,
-    conv_second,
-    point_second,
-    head_second,
-    conv_out,
-    point_out,
-    head_out,
-    second,
-    own_s,
-    got_sz,
-    got_sc,
-    got_sy,
-    got_sx,
-    sem_l,
-    sem_a,
-    sem_p,
-    sem_sz,
-    sem_sc,
-    sem_sy,
-    sem_sx,
-):
-    n_gy, n_gx, _, _ = grid
-    gy, gx = lax.axis_index("gy"), lax.axis_index("gx")
-    ring = ring_size(n_gx)
-    across = n_gx // ring
-    levels = n_gy // 2
-    x, y = gx // ring, lax.rem(gx, ring)
-    z, core = gy // 2, lax.rem(gy, 2)
-    share = chunk.shape[0]
-
-    def level_device(step):
-        return lax.rem(z + step, levels) * 2 + core, gx
-
-    def ring_device(step):
-        return gy, x * ring + lax.rem(y + step, ring)
-
-    def across_device(step):
-        return gy, lax.rem(x + step, across) * ring + y
-
-    def core_device(step):
-        return z * 2 + lax.rem(core + step, 2), gx
-
-    def remote(src, dst, send, recv, device):
-        return pltpu.make_async_remote_copy(
-            src_ref=src,
-            dst_ref=dst,
-            send_sem=send,
-            recv_sem=recv,
-            device_id=device,
-            device_id_type=MESH,
-        )
-
-    def arrival(ref, sem):
-        remote(ref, ref, sem, sem, core_device(1)).wait_recv()
-
-    load = pltpu.make_async_copy(
-        conv_second.at[pl.ds(pl.multiple_of(gy * share, 8), share)], second, sem_l
-    )
-    load.start()
-    barrier = pltpu.get_barrier_semaphore()
-    partners = [ring_device(step) for step in range(1, ring)]
-    partners += [across_device(step) for step in range(1, across)]
-    partners += [level_device(step) for step in range(1, levels)] + [core_device(1)]
-    for device in partners:
-        pl.semaphore_signal(barrier, inc=1, device_id=device, device_id_type=MESH)
-    pl.semaphore_wait(barrier, len(partners))
-
-    started = []
-
-    def go(copy):
-        copy.start()
-        started.append(copy)
-
-    def to_all(value, got, sem, me, device):
-        got[me] = value
-        for step in range(1, got.shape[0]):
-            go(remote(got.at[me], got.at[me], sem.at[0, step], sem.at[1, step], device(step)))
-
-    def gathered(got, sem):
-        for step in range(1, got.shape[0]):
-            arrival(got.at[0], sem.at[1, step])
-        summed = got[0]
-        for k in range(1, got.shape[0]):
-            summed = summed + got[k]
-        return summed
-
-    own_s[...] = jnp.zeros_like(own_s)
-    own_s[0 : point_local.shape[0], :] = point_local[...]
-    own_s[point_local.shape[0] : point_local.shape[0] + 1, :] = head_local[...]
-    to_all(own_s[...], got_sy, sem_sy, y, ring_device)
-    load.wait()
-    conv_out[z * 2 + core] = rms_step(chunk[...], second[...]).astype(BF16)
-    mine = conv_out.at[z * 2 + core]
-    for step in range(1, levels):
-        go(remote(mine, mine, sem_a.at[0, step], sem_a.at[1, step], level_device(step)))
-    go(remote(mine, mine, sem_p.at[0, 0], sem_p.at[1, 0], core_device(1)))
-    to_all(gathered(got_sy, sem_sy), got_sx, sem_sx, x, across_device)
-    small = None
-    for step in range(1, levels):
-        level = lax.rem(z - step + levels, levels)
-        held = conv_out.at[level * 2 + core]
-        arrival(held, sem_a.at[1, step])
-        go(remote(held, held, sem_p.at[0, step], sem_p.at[1, step], core_device(1)))
-        if step == min(2, levels - 1):
-            to_all(gathered(got_sx, sem_sx), got_sc, sem_sc, core, core_device)
-        if step == min(4, levels - 1):
-            to_all(gathered(got_sc, sem_sc), got_sz, sem_sz, z, level_device)
-    small = gathered(got_sz, sem_sz)
-    features = point_local.shape[0]
-    point_out[...] = rms_step(small[:features], point_second[...])
-    head_out[...] = rms_step(small[features : features + 1], head_second[...])
-    for step in range(levels):
-        level = lax.rem(z - step + levels, levels)
-        arrival(conv_out.at[level * 2 + 1 - core], sem_p.at[1, step])
-    for copy in started:
-        copy.wait_send()
-
-
-def finish(grid, chunk, point_local, head_local, conv_second, point_second, head_second):
-    n_gy, n_gx, _, _ = grid
-    share, channels = chunk.shape
-    ring = ring_size(n_gx)
-    across, levels = n_gx // ring, n_gy // 2
-    rows = -(-(point_local.shape[0] + 1) // 8) * 8
-    vmem = pl.BlockSpec(memory_space=pltpu.VMEM)
-    return pl.pallas_call(
-        functools.partial(finish_kernel, grid),
-        out_shape=(
-            jax.ShapeDtypeStruct((n_gy, share, channels), BF16),
-            jax.ShapeDtypeStruct(point_local.shape, F32),
-            jax.ShapeDtypeStruct((1, channels), F32),
-        ),
-        in_specs=[vmem, vmem, vmem, pl.BlockSpec(memory_space=pl.ANY), vmem, vmem],
-        out_specs=(vmem,) * 3,
-        scratch_shapes=[
-            pltpu.VMEM((share, channels), F32),
-            pltpu.VMEM((rows, channels), F32),
-            pltpu.VMEM((levels, rows, channels), F32),
-            pltpu.VMEM((2, rows, channels), F32),
-            pltpu.VMEM((ring, rows, channels), F32),
-            pltpu.VMEM((across, rows, channels), F32),
-            pltpu.SemaphoreType.DMA,
-            pltpu.SemaphoreType.DMA((2, levels)),
-            pltpu.SemaphoreType.DMA((2, levels)),
-            pltpu.SemaphoreType.DMA((2, levels)),
-            pltpu.SemaphoreType.DMA((2, 2)),
-            pltpu.SemaphoreType.DMA((2, ring)),
-            pltpu.SemaphoreType.DMA((2, across)),
-        ],
-        compiler_params=pltpu.CompilerParams(
-            vmem_limit_bytes=VMEM_LIMIT, collective_id=2, has_side_effects=True
-        ),
-        name="finish",
-    )(
-        chunk,
-        point_local,
-        head_local,
+        points,
+        local,
+        point_weight,
+        table,
+        counts,
         conv_second.reshape(n_gy * share, channels),
         point_second,
         head_second.reshape(1, channels),
@@ -915,12 +917,22 @@
     grid = (rows, columns, tile_rows, tile_cols)
 
     pillars, table, local, counts = pool(points, point_pillar, point_weight, slots)
-    returned, kernels, head_local = map_step(
-        grid, pillars, recv_cell, cell_mask, occupancy, conv_weight, head_weight
-    )
-    point_local = point_grad(points, local, point_weight, table, counts, returned)
-    conv_step, point_step, head_step = finish(
-        grid, kernels, point_local, head_local, conv_second, point_second, head_second
+    conv_step, point_step, head_step = map_step(
+        grid,
+        pillars,
+        recv_cell,
+        cell_mask,
+        occupancy,
+        conv_weight,
+        head_weight,
+        points,
+        local,
+        point_weight,
+        table,
+        counts,
+        conv_second,
+        point_second,
+        head_second,
     )
     return conv_step.astype(F32).reshape(conv_second.shape), point_step, head_step[0]
 

time: 127 us -> 107 us (0.84)
  Pallas kernels: 123 us -> 103 us
    pallas_call x2 -> x0, Pallas kernels: 27.3 us -> none  [the longest x1 23.1 us: finish(): pl.pallas_call(functools.partial(finish_kernel, grid), out_shape=(jax.Sha...]
    pallas_call x1, Pallas kernels: 89.2 us -> 96.4 us  [map_step(): pl.pallas_call(functools.partial(map_kernel, grid), out_shape=(jax.ShapeD...]
where the time goes in v2:
time: 107 us
  Pallas kernels  103 us (96%)
  other arithmetic  2.2 us (2%)
  local copies, waits for them, and re-layouts  1.12 us (1%)
    pallas_call x1, Pallas kernels, map_step(): pl.pallas_call(functools.partial(map_kernel, grid), out_shape=(jax.ShapeD...  96.4 us
    pallas_call x1, Pallas kernels, pool(): pl.pallas_call(pool_kernel, out_shape=(jax.ShapeDtypeStruct((slots, chann...  6.29 us
    reshape x1, other arithmetic, on_device(): conv_step.astype(F32).reshape(conv_second.shape)  2.2 us

profile of v2, /device:TPU:1, one launch (start us, length us, event | category | flops | bytes accessed | tf_op | source)
XLA Modules:
  0.0 106.6 jit_solution(13604644211274151179)
XLA Ops:
  0.6 6.3 %pool.1 = (bf16[4096,128]{1,0:T(8,128)(2,1)}, s32[72,128]{1,0:T(8,128)}, s32[32,128]{1,0:T(8,128)}, f32[32,128]{1,0:T(8,128)}) custom-call(bf16[9,4096]{1,0:T(8,128)(2,1)} %points.3, s32[32,128]{1,0:T(8,128)} %bitcast.15, s32[1,4096]{1,0:T(1,128)} %bitcast.16, bf16[9,128]{1,0:T(8,128)(2,1)} %point_weight.1), custom_call_target="tpu_custom_call" | custom-call | tf_op jit(solution)/shard_map/pool/pallas_call | solution.py:108
  6.9 96.4 %map_step.1 = (bf16[16,144,128]{2,1,0:T(8,128)(2,1)}, f32[9,128]{1,0:T(8,128)}, f32[1,128]{1,0:T(1,128)}) custom-call(bf16[4096,128]{1,0:T(8,128)(2,1)} %get-tuple-element.10.pillars, s32[32,128]{1,0:T(8,128)} %bitcast.17, s32[16,32]{1,0:T(8,128)} %bitcast.18, s32[16,32]{1,0:T(8,128)} %bitcast.19, bf16[2,1152,128]{2,1,0:T(8,128)(2,1)} %bitcast.14, ...), custom_call_target="tpu_custom_call" | custom-call | tf_op jit(solution)/shard_map/map_step/pallas_call | solution.py:812
  103.3 0.0 copy-start
  103.3 0.0 copy-start.1
  103.3 2.2 %convert.1 = f32[2,9,128,128]{3,2,1,0:T(8,128)} convert(bf16[2,9,128,128]{3,2,1,0:T(8,128)(2,1)} %bitcast.13) | non-fusion elementwise | flops 294912 | bytes 1769472 | tf_op jit(solution)/shard_map/reshape | solution.py:937
  105.5 0.0 copy-done
  105.5 0.6 copy.16
  106.1 0.0 copy-done.1
  106.1 0.5 copy.17
Async XLA Ops:
  103.3 2.2 %copy-start = (f32[9,128]{1,0:T(8,128)S(1)}, f32[9,128]{1,0:T(8,128)}, u32[]{:S(2)}) copy-start(f32[9,128]{1,0:T(8,128)} %get-tuple-element.21) | copy-start | bytes 13828
  103.3 2.8 %copy-start.1 = (f32[1,128]{1,0:T(1,128)S(1)}, f32[1,128]{1,0:T(1,128)}, u32[]{:S(2)}) copy-start(f32[1,128]{1,0:T(1,128)} %get-tuple-element.16) | copy-start | bytes 1540

commit v3 on v2

--- a/solution.py
+++ b/solution.py
@@ -221,6 +221,10 @@
     sem_sx,
     sem_sz,
     sem_l,
+    pass_x,
+    pass_r,
+    sem_px,
+    sem_pr,
 ):
     n_gy, n_gx, tile_rows, tile_cols = grid
     gy, gx = lax.axis_index("gy"), lax.axis_index("gx")
@@ -305,17 +309,28 @@
         copy.start()
         started.append(copy)
 
+    def between(r):
+        if across != 4:
+            return 0
+        return 1 if r % 2 == 0 else -1
+
     def send_pillars(r):
-        for o in range(1, across):
-            go(
-                remote(
-                    pillars.at[slot_block(over(o), along(order[r]))],
-                    got_x.at[pl.ds((r * across + o) * CHUNK, CHUNK)],
-                    sem_x.at[0, r, o],
-                    sem_x.at[1, r, o],
-                    across_device(o),
-                )
-            )
+        for o in (2, 1, 3) if between(r) else range(1, across):
+            src = pillars.at[slot_block(over(o), along(order[r]))]
+            dst = got_x.at[pl.ds((r * across + o) * CHUNK, CHUNK)]
+            if o == 2 and between(r):
+                device = across_device(between(r))
+                go(remote(src, pass_x.at[r], sem_x.at[0, r, o], sem_px.at[1, r], device))
+            else:
+                device = across_device(o)
+                go(remote(src, dst, sem_x.at[0, r, o], sem_x.at[1, r, o], device))
+
+    def pass_pillars(r):
+        if between(r):
+            arrival(pass_x.at[r], sem_px.at[1, r])
+            dst = got_x.at[pl.ds((r * across + 2) * CHUNK, CHUNK)]
+            device = across_device(between(r))
+            go(remote(pass_x.at[r], dst, sem_px.at[0, r], sem_x.at[1, r, 2], device))
 
     for r in range(min(3, ring)):
         send_pillars(r)
@@ -477,6 +492,7 @@
         for r in range(2 * t + 1, min(2 * t + 3, ring)) if t else ():
             send_pillars(r)
         if t == 0:
+            pass_pillars(0)
             build_place(0)
             summed = placed_for(0)
             for side in (0, 1):
@@ -494,6 +510,8 @@
                     half = 1 - side if order_half == 0 else side
                     if t > 1 or half == side:
                         grow(t, side, half, half_of(summed[side], half))
+        for r in range(2 * t + 1, min(2 * t + 3, ring)):
+            pass_pillars(r)
         for r in left[:2]:
             build_pick(r)
         left = left[2:]
@@ -565,21 +583,31 @@
             )
         )
 
+    def passes(r):
+        return between(r) and r != slot_of[half_ring]
+
     def hand_out(rel, gradient):
         r = slot_of[rel]
         rows = dot(pick[r], gradient).astype(BF16)
         returned[slot_block(x, along(rel)), :] = rows[:CHUNK]
         send_r[r] = rows
-        for o in range(1, across):
-            go(
-                remote(
-                    send_r.at[r, pl.ds(o * CHUNK, CHUNK)],
-                    returned.at[slot_block(x, along(rel))],
-                    sem_r.at[0, r, o],
-                    sem_r.at[1, r, o],
-                    across_device(-o),
-                )
-            )
+        for o in (2, 1, 3) if passes(r) else range(1, across):
+            src = send_r.at[r, pl.ds(o * CHUNK, CHUNK)]
+            if o == 2 and passes(r):
+                device = across_device(between(r))
+                go(remote(src, pass_r.at[r], sem_r.at[0, r, o], sem_pr.at[1, r], device))
+            else:
+                dst = returned.at[slot_block(x, along(rel))]
+                device = across_device(-o)
+                go(remote(src, dst, sem_r.at[0, r, o], sem_r.at[1, r, o], device))
+
+    def pass_back(rel):
+        r = slot_of[rel]
+        if passes(r):
+            arrival(pass_r.at[r], sem_pr.at[1, r])
+            device = across_device(between(r))
+            dst = returned.at[slot_block(over(-between(r)), along(rel))]
+            go(remote(pass_r.at[r], dst, sem_pr.at[0, r], sem_r.at[1, r, 2], device))
 
     parts = levels // 2
 
@@ -713,11 +741,16 @@
     for order_half in (0, 1):
         for side in (0, 1):
             pass_on(1, side, side if order_half == 0 else 1 - side)
+    hand_out(0, own_g[...])
     own1 = (cut(grad1, 1, tile_rows) * own_column).astype(BF16)
     halve(0, dot_tn(windows(v0, 3, tile_rows), own1))
-    own2 = (cut(grad2, 2, tile_rows) * own_column).astype(BF16)
-    halve(1, dot_tn(windows(v1, 2, tile_rows), own2))
-    hand_out(0, own_g[...])
+
+    def second_kernel():
+        own2 = (cut(grad2, 2, tile_rows) * own_column).astype(BF16)
+        halve(1, dot_tn(windows(v1, 2, tile_rows), own2))
+
+    if half_ring == 1:
+        second_kernel()
     head_terms = cut(logit_grad * hidden2.astype(F32), 2, tile_rows) * own_column
     head_local = jnp.sum(head_terms, axis=0, keepdims=True)
     prepared = 0
@@ -732,10 +765,9 @@
         else:
             for side in (0, 1):
                 arrival(got_g.at[side, t - 1, halves[side]], sem_g.at[1, side, t - 1, side])
-        if t == 1:
+        if t == min(2, half_ring):
             to_levels()
         if t == half_ring:
-            to_pieces(gathered(got_kz, sem_kz))
             hand_out(
                 t,
                 jnp.concatenate(
@@ -745,6 +777,12 @@
         else:
             hand_out(-t, got_g[0, t - 1])
             hand_out(t, got_g[1, t - 1])
+            if t == 1:
+                second_kernel()
+        for rel in (0,) if t == 1 else (1 - t, t - 1):
+            pass_back(rel)
+        if t == half_ring:
+            to_pieces(gathered(got_kz, sem_kz))
         share_to = chunks * t // half_ring
         prepare(prepared, share_to)
         prepared = share_to
@@ -874,6 +912,10 @@
             pltpu.SemaphoreType.DMA((2, across)),
             pltpu.SemaphoreType.DMA((2, n_gy)),
             pltpu.SemaphoreType.DMA,
+            pltpu.VMEM((ring, CHUNK, channels), BF16),
+            pltpu.VMEM((ring, CHUNK, channels), BF16),
+            pltpu.SemaphoreType.DMA((2, ring)),
+            pltpu.SemaphoreType.DMA((2, ring)),
         ],
         compiler_params=pltpu.CompilerParams(
             vmem_limit_bytes=VMEM_LIMIT, collective_id=1, has_side_effects=True

time: 107 us -> 117 us (1.093)
  Pallas kernels: 103 us -> 113 us
    pallas_call x1, Pallas kernels: 96.4 us -> 106 us  [map_step(): pl.pallas_call(functools.partial(map_kernel, grid), out_shape=(jax.ShapeD...]
where the time goes in v3:
time: 117 us
  Pallas kernels  113 us (97%)
  other arithmetic  2.2 us (2%)
    pallas_call x1, Pallas kernels, map_step(): pl.pallas_call(functools.partial(map_kernel, grid), out_shape=(jax.ShapeD...  106 us
    pallas_call x1, Pallas kernels, pool(): pl.pallas_call(pool_kernel, out_shape=(jax.ShapeDtypeStruct((slots, chann...  6.28 us

profile of v3, /device:TPU:1, one launch (start us, length us, event | category | flops | bytes accessed | tf_op | source)
XLA Modules:
  0.0 116.6 jit_solution(14330785950134939613)
XLA Ops:
  0.6 6.3 %pool.1 = (bf16[4096,128]{1,0:T(8,128)(2,1)}, s32[72,128]{1,0:T(8,128)}, s32[32,128]{1,0:T(8,128)}, f32[32,128]{1,0:T(8,128)}) custom-call(bf16[9,4096]{1,0:T(8,128)(2,1)} %points.3, s32[32,128]{1,0:T(8,128)} %bitcast.15, s32[1,4096]{1,0:T(1,128)} %bitcast.16, bf16[9,128]{1,0:T(8,128)(2,1)} %point_weight.1), custom_call_target="tpu_custom_call" | custom-call | tf_op jit(solution)/shard_map/pool/pallas_call | solution.py:108
  6.9 106.3 %map_step.1 = (bf16[16,144,128]{2,1,0:T(8,128)(2,1)}, f32[9,128]{1,0:T(8,128)}, f32[1,128]{1,0:T(1,128)}) custom-call(bf16[4096,128]{1,0:T(8,128)(2,1)} %get-tuple-element.10.pillars, s32[32,128]{1,0:T(8,128)} %bitcast.17, s32[16,32]{1,0:T(8,128)} %bitcast.18, s32[16,32]{1,0:T(8,128)} %bitcast.19, bf16[2,1152,128]{2,1,0:T(8,128)(2,1)} %bitcast.14, ...), custom_call_target="tpu_custom_call" | custom-call | tf_op jit(solution)/shard_map/map_step/pallas_call | solution.py:850
  113.2 0.0 copy-start
  113.2 0.0 copy-start.1
  113.3 2.2 %convert.1 = f32[2,9,128,128]{3,2,1,0:T(8,128)} convert(bf16[2,9,128,128]{3,2,1,0:T(8,128)(2,1)} %bitcast.13) | non-fusion elementwise | flops 294912 | bytes 1769472 | tf_op jit(solution)/shard_map/reshape | solution.py:979
  115.5 0.0 copy-done
  115.5 0.6 copy.16
  116.1 0.0 copy-done.1
  116.1 0.5 copy.17
Async XLA Ops:
  113.2 2.2 %copy-start = (f32[9,128]{1,0:T(8,128)S(1)}, f32[9,128]{1,0:T(8,128)}, u32[]{:S(2)}) copy-start(f32[9,128]{1,0:T(8,128)} %get-tuple-element.21) | copy-start | bytes 13828
  113.2 2.8 %copy-start.1 = (f32[1,128]{1,0:T(1,128)S(1)}, f32[1,128]{1,0:T(1,128)}, u32[]{:S(2)}) copy-start(f32[1,128]{1,0:T(1,128)} %get-tuple-element.16) | copy-start | bytes 1540

commit v4 on v2

--- a/solution.py
+++ b/solution.py
@@ -14,6 +14,7 @@
 CHUNK = 128
 SIDE = 8
 HALO = 4
+PARTS = 4
 STEPS = ((0, -1), (0, 1), (-1, 0), (1, 0), (-1, -1), (1, 1), (-1, 1), (1, -1))
 
 
@@ -137,11 +138,11 @@
 
 
 def ring_size(columns):
-    return {32: 8, 8: 4, 4: 2}[columns]
+    return 8 if columns % 16 == 0 else columns
 
 
 def ring_order(ring):
-    order = [ring // 2]
+    order = []
     for far in range(ring // 2 - 1, 0, -1):
         order += [far, -far]
     return order + [0]
@@ -221,6 +222,12 @@
     sem_sx,
     sem_sz,
     sem_l,
+    got_far,
+    send_far,
+    place_far,
+    pick_far,
+    sem_far,
+    sem_back,
 ):
     n_gy, n_gx, tile_rows, tile_cols = grid
     gy, gx = lax.axis_index("gy"), lax.axis_index("gx")
@@ -229,14 +236,15 @@
     half_ring = ring // 2
     order = ring_order(ring)
     slot_of = {rel: r for r, rel in enumerate(order)}
-    slot_of[-half_ring] = slot_of[half_ring]
+    middle = half_ring // 2
+    half_block = CHUNK // 2
     x, y = gx // ring, lax.rem(gx, ring)
     channels = pillars.shape[1]
     spans, _ = message_rows(tile_rows, tile_cols)
     width = tile_cols + 2 * SIDE
     height = tile_rows + 2 * HALO
     count = tile_rows * tile_cols
-    part_rows = count // 2
+    part_rows = count // PARTS
     fan = across * CHUNK
 
     def neighbour(k):
@@ -265,6 +273,14 @@
 
     def stack_device(step):
         return lax.rem(gy + step, n_gy), gx
+
+    def slot_half(column, place_on_ring, side):
+        at = (column * ring + place_on_ring) * CHUNK + side * half_block
+        return pl.ds(pl.multiple_of(at, half_block), half_block)
+
+    def middle_device(o, side):
+        away = half_ring - middle if side == 0 else middle - half_ring
+        return gy, over(o) * ring + along(away)
 
     def slot_block(column, place_on_ring):
         return pl.ds(pl.multiple_of((column * ring + place_on_ring) * CHUNK, CHUNK), CHUNK)
@@ -295,6 +311,7 @@
     partners += [ring_device(step) for step in range(1, ring)]
     partners += [across_device(step) for step in range(1, across)]
     partners += [stack_device(step) for step in range(1, n_gy)]
+    partners += [middle_device(o, side) for o in range(1, across) for side in (0, 1)]
     for device in partners:
         pl.semaphore_signal(barrier, inc=1, device_id=device, device_id_type=MESH)
     pl.semaphore_wait(barrier, len(partners))
@@ -317,8 +334,19 @@
                 )
             )
 
-    for r in range(min(3, ring)):
+    for r in (0, 1):
         send_pillars(r)
+    for side in (0, 1):
+        for o in range(across):
+            go(
+                remote(
+                    pillars.at[slot_half(over(o), along(half_ring), side)],
+                    got_far.at[side, pl.ds(o * half_block, half_block)],
+                    sem_far.at[0, side, o],
+                    sem_far.at[1, side, o],
+                    middle_device(o, side),
+                )
+            )
 
     send_i[...] = jnp.zeros_like(send_i)
     for step in range(ring):
@@ -326,11 +354,12 @@
         for o in range(across):
             row = over(-o) * ring + along(step)
             send_i[lead + o : lead + o + 1, :] = cells[pl.ds(row, 1), :]
+            row = over(-o) * ring + along(half_ring)
+            send_i[lead + 4 + o : lead + 5 + o, :] = cells[pl.ds(row, 1), :]
         if step == 0:
             got_i[pl.ds(slot_of[0] * 8, 8), :] = send_i[pl.ds(0, 8), :]
-        else:
-            rel = -step if step <= half_ring else ring - step
-            slot = slot_of[rel]
+        elif step != half_ring:
+            slot = slot_of[-step if step < half_ring else ring - step]
             go(
                 remote(
                     send_i.at[pl.ds(lead, 8)],
@@ -405,9 +434,9 @@
     column = iota((tile_rows * width, channels), 0) % width
     own_column = jnp.where((column >= SIDE) & (column < SIDE + tile_cols), 1.0, 0.0)
 
-    for r in range(ring - 1):
+    for r in range(len(order) - 1):
         arrival(got_i.at[pl.ds(r * 8, 8)], sem_i.at[1, r])
-    rows_i = ring * 8
+    rows_i = len(order) * 8
     cells_i = got_i[...]
     cells_t = jnp.concatenate(
         [cells_i.astype(F32), jnp.zeros(((-rows_i) % CHUNK, CHUNK), F32)], axis=0
@@ -426,6 +455,24 @@
                 cells_t[:, at : at + 1] == iota((CHUNK, count), 1), 1.0, 0.0
             ).astype(BF16)
 
+    def build_far(side):
+        lead = slot_of[middle if side == 0 else -middle] * 8 + 4
+        lower = iota((1, CHUNK), 1) < half_block
+        for o in range(0, across, 2):
+            one, two = (cells_i[at : at + 1, :] for at in (lead + o, lead + o + 1))
+            if side == 0:
+                two = pltpu.roll(two, half_block, axis=1)
+            else:
+                one = pltpu.roll(one, half_block, axis=1)
+            place_far[side, :, pl.ds(o * half_block, CHUNK)] = jnp.where(
+                iota((count, CHUNK), 0) == jnp.where(lower, one, two), 1.0, 0.0
+            ).astype(BF16)
+        for o in range(across):
+            rows = cells_t[side * half_block : (side + 1) * half_block, lead + o : lead + o + 1]
+            pick_far[side, pl.ds(o * half_block, half_block), :] = jnp.where(
+                rows == iota((half_block, count), 1), 1.0, 0.0
+            ).astype(BF16)
+
     def cut(value, lead, rows):
         return value[lead * width : (lead + rows) * width]
 
@@ -452,48 +499,45 @@
         rest = got_x[pl.ds((r * across + 1) * CHUNK, fan - CHUNK), :]
         return dot(place[r], jnp.concatenate([own, rest], axis=0))
 
-    halves = (pl.ds(0, part_rows), pl.ds(part_rows, part_rows))
-
-    def half_of(value, half):
-        return value[half * part_rows : (half + 1) * part_rows]
-
-    def grow(t, side, half, value):
-        if t > 1 or (t == 1 and half == side):
-            arrival(got_y.at[side, t - 1, halves[half]], sem_y.at[1, side, t - 1, half])
-            value = value + got_y[side, t - 1, halves[half], :].astype(F32)
-        send_y[side, t, halves[half], :] = value.astype(BF16)
+    pieces = [pl.ds(q * part_rows, part_rows) for q in range(PARTS)]
+
+    def grow(t, side, q, value):
+        if t:
+            arrival(got_y.at[side, t - 1, pieces[q]], sem_y.at[1, side, t - 1, q])
+            value = value + got_y[side, t - 1, pieces[q], :].astype(F32)
+        send_y[side, t, pieces[q], :] = value.astype(BF16)
         go(
             remote(
-                send_y.at[side, t, halves[half]],
-                got_y.at[side, t, halves[half]],
-                sem_y.at[0, side, t, half],
-                sem_y.at[1, side, t, half],
+                send_y.at[side, t, pieces[q]],
+                got_y.at[side, t, pieces[q]],
+                sem_y.at[0, side, t, q],
+                sem_y.at[1, side, t, q],
                 ring_device(1 - 2 * side),
             )
         )
 
-    left = list(range(ring))
-    for t in range(half_ring):
-        for r in range(2 * t + 1, min(2 * t + 3, ring)) if t else ():
+    left = list(range(len(order)))
+    for t in range(half_ring - 1):
+        for r in range(2 * t + 2, min(2 * t + 4, len(order))):
             send_pillars(r)
-        if t == 0:
-            build_place(0)
-            summed = placed_for(0)
+        summed = {}
+        for side in (0, 1):
+            away = half_ring - 1 - t
+            r = slot_of[away if side == 0 else -away]
+            build_place(r)
+            if away == middle:
+                build_far(side)
+            value = placed_for(r)
+            if away == middle:
+                for o in range(across):
+                    arrival(
+                        got_far.at[side, pl.ds(o * half_block, half_block)], sem_far.at[1, side, o]
+                    )
+                value = value + dot(place_far[side], got_far[side])
+            summed[side] = value
+        for q in range(PARTS):
             for side in (0, 1):
-                grow(0, side, side, half_of(summed, side))
-        else:
-            summed = {}
-            for side in (0, 1):
-                r = slot_of[(1 - 2 * side) * (half_ring - t)]
-                build_place(r)
-                summed[side] = placed_for(r)
-                if t == 1:
-                    grow(t, side, 1 - side, half_of(summed[side], 1 - side))
-            for order_half in (0, 1):
-                for side in (0, 1):
-                    half = 1 - side if order_half == 0 else side
-                    if t > 1 or half == side:
-                        grow(t, side, half, half_of(summed[side], half))
+                grow(t, side, q, summed[side][q * part_rows : (q + 1) * part_rows])
         for r in left[:2]:
             build_pick(r)
         left = left[2:]
@@ -517,16 +561,32 @@
         :, SIDE : SIDE + tile_cols
     ].reshape(count, channels)
 
-    last = half_ring - 1
+    last = half_ring - 2
     ends = []
-    for half in (0, 1):
-        value = half_of(placed, half)
+    for q in range(PARTS):
+        value = placed[q * part_rows : (q + 1) * part_rows]
         for side in (0, 1):
-            if last or half == side:
-                arrival(got_y.at[side, last, halves[half]], sem_y.at[1, side, last, half])
-                value = value + got_y[side, last, halves[half], :].astype(F32)
+            arrival(got_y.at[side, last, pieces[q]], sem_y.at[1, side, last, q])
+            value = value + got_y[side, last, pieces[q], :].astype(F32)
         ends.append(value)
     placed = jnp.concatenate(ends, axis=0)
+
+    parts = levels // 2
+
+    def halve(layer, gradient):
+        own_k[pl.ds(layer * parts, parts)] = gradient.reshape(
+            parts, 2, share, channels
+        ).astype(BF16)
+        go(
+            remote(
+                own_k.at[pl.ds(layer * parts, parts), 1 - core],
+                core_k.at[pl.ds(layer * parts, parts)],
+                sem_c.at[0, layer],
+                sem_c.at[1, layer],
+                other_core,
+            )
+        )
+
     features = (placed * visible).astype(BF16).astype(F32)
     post(features, send_f, got_f, sem_f)
     side_by_side(collect(features, got_f, sem_f) * in_slab, v0)
@@ -544,26 +604,44 @@
     ) / cells_all
     grad2 = logit_grad * head_row[...].astype(F32) * (sig2 * (1.0 + pre2 * (1.0 - sig2)))
     side_by_side(grad2, v2)
+    own2 = (cut(grad2, 2, tile_rows) * own_column).astype(BF16)
+    halve(1, dot_tn(windows(v1, 2, tile_rows), own2))
     back2 = dot_nt(windows(v2, 0, height - 6), flipped(1))
     grad1 = back2 * slope(cut(pre1, 2, height - 6)) * cut(in_slab, 3, height - 6)
     side_by_side(grad1, v3)
+    own1 = (cut(grad1, 1, tile_rows) * own_column).astype(BF16)
+    halve(0, dot_tn(windows(v0, 3, tile_rows), own1))
     back1 = dot_nt(windows(v3, 0, tile_rows), flipped(0))
     back1 = back1.reshape(tile_rows, width, channels)[:, SIDE : SIDE + tile_cols].reshape(
         count, channels
     )
     own_g[...] = (back1 * visible).astype(BF16)
 
-    def pass_on(t, side, half):
+    def pass_on(t, side, q):
         src = own_g if t == 1 else got_g.at[side, t - 2]
         go(
             remote(
-                src.at[halves[half]],
-                got_g.at[side, t - 1, halves[half]],
-                sem_g.at[0, side, t - 1, half],
-                sem_g.at[1, side, t - 1, half],
+                src.at[pieces[q]],
+                got_g.at[side, t - 1, pieces[q]],
+                sem_g.at[0, side, t - 1, q],
+                sem_g.at[1, side, t - 1, q],
                 ring_device(1 - 2 * side),
             )
         )
+
+    def hand_far(side, gradient):
+        rel = middle if side == 0 else -middle
+        send_far[side] = dot(pick_far[side], gradient).astype(BF16)
+        for o in range(across):
+            go(
+                remote(
+                    send_far.at[side, pl.ds(o * half_block, half_block)],
+                    returned.at[slot_half(x, along(rel), side)],
+                    sem_back.at[0, side, o],
+                    sem_back.at[1, side, o],
+                    middle_device(-o, 1 - side),
+                )
+            )
 
     def hand_out(rel, gradient):
         r = slot_of[rel]
@@ -580,22 +658,6 @@
                     across_device(-o),
                 )
             )
-
-    parts = levels // 2
-
-    def halve(layer, gradient):
-        own_k[pl.ds(layer * parts, parts)] = gradient.reshape(
-            parts, 2, share, channels
-        ).astype(BF16)
-        go(
-            remote(
-                own_k.at[pl.ds(layer * parts, parts), 1 - core],
-                core_k.at[pl.ds(layer * parts, parts)],
-                sem_c.at[0, layer],
-                sem_c.at[1, layer],
-                other_core,
-            )
-        )
 
     def to_levels():
         for layer in (0, 1):
@@ -710,52 +772,42 @@
             rows_b[part, :] = (dot(picks[part, :], window) * slopes[part, :]).astype(BF16)
         return dot(points[...], rows_b[...])
 
-    for order_half in (0, 1):
+    for q in range(PARTS):
         for side in (0, 1):
-            pass_on(1, side, side if order_half == 0 else 1 - side)
-    own1 = (cut(grad1, 1, tile_rows) * own_column).astype(BF16)
-    halve(0, dot_tn(windows(v0, 3, tile_rows), own1))
-    own2 = (cut(grad2, 2, tile_rows) * own_column).astype(BF16)
-    halve(1, dot_tn(windows(v1, 2, tile_rows), own2))
+            pass_on(1, side, q)
     hand_out(0, own_g[...])
+    to_levels()
     head_terms = cut(logit_grad * hidden2.astype(F32), 2, tile_rows) * own_column
     head_local = jnp.sum(head_terms, axis=0, keepdims=True)
     prepared = 0
-    for t in range(1, half_ring + 1):
-        if t < half_ring:
-            for order_half in (0, 1):
-                for side in (0, 1):
-                    half = side if order_half == 0 else 1 - side
-                    arrival(got_g.at[side, t - 1, halves[half]], sem_g.at[1, side, t - 1, half])
-                    if t + 1 < half_ring or order_half == 0:
-                        pass_on(t + 1, side, half)
-        else:
+    for t in range(1, half_ring):
+        for q in range(PARTS):
             for side in (0, 1):
-                arrival(got_g.at[side, t - 1, halves[side]], sem_g.at[1, side, t - 1, side])
-        if t == 1:
-            to_levels()
-        if t == half_ring:
-            to_pieces(gathered(got_kz, sem_kz))
-            hand_out(
-                t,
-                jnp.concatenate(
-                    [got_g[side, t - 1, halves[side], :] for side in (0, 1)], axis=0
-                ),
-            )
-        else:
-            hand_out(-t, got_g[0, t - 1])
-            hand_out(t, got_g[1, t - 1])
-        share_to = chunks * t // half_ring
+                arrival(got_g.at[side, t - 1, pieces[q]], sem_g.at[1, side, t - 1, q])
+                if t + 1 < half_ring:
+                    pass_on(t + 1, side, q)
+        if t == middle:
+            hand_far(0, got_g[1, t - 1])
+            hand_far(1, got_g[0, t - 1])
+        hand_out(-t, got_g[0, t - 1])
+        hand_out(t, got_g[1, t - 1])
+        share_to = chunks * t // (half_ring - 1)
         prepare(prepared, share_to)
         prepared = share_to
-    to_all(gathered(got_kx, sem_kx), got_ky, sem_ky, y, ring_device)
+    to_pieces(gathered(got_kz, sem_kz))
     for r, rel in enumerate(order):
         for o in range(1, across):
             arrival(returned.at[slot_block(over(o), along(rel))], sem_r.at[1, r, o])
+    for side in (0, 1):
+        for o in range(across):
+            arrival(
+                returned.at[slot_half(over(o), along(half_ring), side)], sem_back.at[1, side, o]
+            )
     start_merge()
-    merge(0, min(2, levels_m))
+    to_all(gathered(got_kx, sem_kx), got_ky, sem_ky, y, ring_device)
+    merge(0, min(3, levels_m))
     to_all(take_step(gathered(got_ky, sem_ky)), got_ax, sem_ax, x, across_device)
-    merge(min(2, levels_m), levels_m)
+    merge(min(3, levels_m), levels_m)
     for step in range(1, across):
         arrival(got_ax.at[0], sem_ax.at[1, step])
     conv_out[gy] = got_ax[...].reshape(across * piece, channels)[:share]
@@ -819,8 +871,8 @@
         in_specs=[vmem] * 9 + [smem, vmem, pl.BlockSpec(memory_space=pl.ANY), vmem, vmem],
         out_specs=(vmem,) * 3,
         scratch_shapes=[
-            pltpu.VMEM((ring, count, across * CHUNK), BF16),
-            pltpu.VMEM((ring, across * CHUNK, count), BF16),
+            pltpu.VMEM((ring - 1, count, across * CHUNK), BF16),
+            pltpu.VMEM((ring - 1, across * CHUNK, count), BF16),
             pltpu.VMEM((rows, channels), BF16),
             pltpu.VMEM((rows, channels), BF16),
             pltpu.VMEM((rows, channels), BF16),
@@ -830,13 +882,13 @@
             pltpu.VMEM(((height - 4) * width, 3 * channels), BF16),
             pltpu.VMEM(((height - 6) * width, 3 * channels), BF16),
             pltpu.VMEM((ring * 8, CHUNK), jnp.int32),
-            pltpu.VMEM((ring * 8, CHUNK), jnp.int32),
-            pltpu.VMEM((slots, channels), BF16),
-            pltpu.VMEM((2, half_ring, count, channels), BF16),
-            pltpu.VMEM((2, half_ring, count, channels), BF16),
+            pltpu.VMEM(((ring - 1) * 8, CHUNK), jnp.int32),
+            pltpu.VMEM(((ring - 1) * across * CHUNK, channels), BF16),
+            pltpu.VMEM((2, half_ring - 1, count, channels), BF16),
+            pltpu.VMEM((2, half_ring - 1, count, channels), BF16),
             pltpu.VMEM((count, channels), BF16),
-            pltpu.VMEM((2, half_ring, count, channels), BF16),
-            pltpu.VMEM((ring, across * CHUNK, channels), BF16),
+            pltpu.VMEM((2, half_ring - 1, count, channels), BF16),
+            pltpu.VMEM((ring - 1, across * CHUNK, channels), BF16),
             pltpu.VMEM((slots, channels), BF16),
             pltpu.VMEM((levels, 2, share, channels), BF16),
             pltpu.VMEM((levels, share, channels), BF16),
@@ -860,8 +912,8 @@
             pltpu.SemaphoreType.DMA((2, len(STEPS))),
             pltpu.SemaphoreType.DMA((2, ring)),
             pltpu.SemaphoreType.DMA((2, ring, across)),
-            pltpu.SemaphoreType.DMA((2, 2, half_ring, 2)),
-            pltpu.SemaphoreType.DMA((2, 2, half_ring, 2)),
+            pltpu.SemaphoreType.DMA((2, 2, half_ring - 1, PARTS)),
+            pltpu.SemaphoreType.DMA((2, 2, half_ring - 1, PARTS)),
             pltpu.SemaphoreType.DMA((2, ring, across)),
             pltpu.SemaphoreType.DMA((2, 2)),
             pltpu.SemaphoreType.DMA((2, levels)),
@@ -874,6 +926,12 @@
             pltpu.SemaphoreType.DMA((2, across)),
             pltpu.SemaphoreType.DMA((2, n_gy)),
             pltpu.SemaphoreType.DMA,
+            pltpu.VMEM((2, across * CHUNK // 2, channels), BF16),
+            pltpu.VMEM((2, across * CHUNK // 2, channels), BF16),
+            pltpu.VMEM((2, count, across * CHUNK // 2), BF16),
+            pltpu.VMEM((2, across * CHUNK // 2, count), BF16),
+            pltpu.SemaphoreType.DMA((2, 2, across)),
+            pltpu.SemaphoreType.DMA((2, 2, across)),
         ],
         compiler_params=pltpu.CompilerParams(
             vmem_limit_bytes=VMEM_LIMIT, collective_id=1, has_side_effects=True

time: 107 us -> 111 us (1.037)
  Pallas kernels: 103 us -> 107 us
    pallas_call x1, Pallas kernels: 96.4 us -> 100 us  [map_step(): pl.pallas_call(functools.partial(map_kernel, grid), out_shape=(jax.ShapeD...]
where the time goes in v4:
time: 111 us
  Pallas kernels  107 us (96%)
  other arithmetic  2.2 us (2%)
  local copies, waits for them, and re-layouts  1.12 us (1%)
    pallas_call x1, Pallas kernels, map_step(): pl.pallas_call(functools.partial(map_kernel, grid), out_shape=(jax.ShapeD...  100 us
    pallas_call x1, Pallas kernels, pool(): pl.pallas_call(pool_kernel, out_shape=(jax.ShapeDtypeStruct((slots, chann...  6.28 us

profile of v4, /device:TPU:1, one launch (start us, length us, event | category | flops | bytes accessed | tf_op | source)
XLA Modules:
  0.0 110.6 jit_solution(7872347779857767639)
XLA Ops:
  0.6 6.3 %pool.1 = (bf16[4096,128]{1,0:T(8,128)(2,1)}, s32[72,128]{1,0:T(8,128)}, s32[32,128]{1,0:T(8,128)}, f32[32,128]{1,0:T(8,128)}) custom-call(bf16[9,4096]{1,0:T(8,128)(2,1)} %points.3, s32[32,128]{1,0:T(8,128)} %bitcast.15, s32[1,4096]{1,0:T(1,128)} %bitcast.16, bf16[9,128]{1,0:T(8,128)(2,1)} %point_weight.1), custom_call_target="tpu_custom_call" | custom-call | tf_op jit(solution)/shard_map/pool/pallas_call | solution.py:109
  6.9 100.3 %map_step.1 = (bf16[16,144,128]{2,1,0:T(8,128)(2,1)}, f32[9,128]{1,0:T(8,128)}, f32[1,128]{1,0:T(1,128)}) custom-call(bf16[4096,128]{1,0:T(8,128)(2,1)} %get-tuple-element.10.pillars, s32[32,128]{1,0:T(8,128)} %bitcast.17, s32[16,32]{1,0:T(8,128)} %bitcast.18, s32[16,32]{1,0:T(8,128)} %bitcast.19, bf16[2,1152,128]{2,1,0:T(8,128)(2,1)} %bitcast.14, ...), custom_call_target="tpu_custom_call" | custom-call | tf_op jit(solution)/shard_map/map_step/pallas_call | solution.py:864
  107.2 0.0 copy-start
  107.2 0.0 copy-start.1
  107.3 2.2 %convert.1 = f32[2,9,128,128]{3,2,1,0:T(8,128)} convert(bf16[2,9,128,128]{3,2,1,0:T(8,128)(2,1)} %bitcast.13) | non-fusion elementwise | flops 294912 | bytes 1769472 | tf_op jit(solution)/shard_map/reshape | solution.py:995
  109.5 0.0 copy-done
  109.5 0.6 copy.16
  110.1 0.0 copy-done.1
  110.1 0.5 copy.17
Async XLA Ops:
  107.2 2.2 %copy-start = (f32[9,128]{1,0:T(8,128)S(1)}, f32[9,128]{1,0:T(8,128)}, u32[]{:S(2)}) copy-start(f32[9,128]{1,0:T(8,128)} %get-tuple-element.21) | copy-start | bytes 13828
  107.2 2.8 %copy-start.1 = (f32[1,128]{1,0:T(1,128)S(1)}, f32[1,128]{1,0:T(1,128)}, u32[]{:S(2)}) copy-start(f32[1,128]{1,0:T(1,128)} %get-tuple-element.16) | copy-start | bytes 1540

commit v5 on v2

--- a/solution.py
+++ b/solution.py
@@ -43,7 +43,26 @@
     return gradient / (jnp.sqrt(moment) + 1e-08)
 
 
+def ring_size(columns):
+    return {32: 8, 8: 4, 4: 2}[columns]
+
+
+def tile_places(columns):
+    ring = ring_size(columns)
+    across = columns // ring
+    gx = lax.axis_index("gx")
+    x, y = gx // ring, lax.rem(gx, ring)
+
+    def rows(d):
+        away = lax.rem(d // ring - x + across, across)
+        place = lax.rem(d % ring - y + ring + ring // 2 - 1, ring)
+        return pl.ds(pl.multiple_of((away * ring + place) * CHUNK, CHUNK), CHUNK)
+
+    return rows
+
+
 def pool_kernel(
+    columns,
     points, ids, ids_row, weight, pillars, table, local, counts, table_s, partial, sums, numbers, sem
 ):
     chunks = ids.shape[0]
@@ -89,24 +108,25 @@
             first_rows = got[0:8] if k == 0 else compact[pl.ds(at, 8), :] + got[0:8]
             compact[pl.ds(at, CHUNK + 8), :] = jnp.concatenate([first_rows, got[8:], edge], axis=0)
     diagonal = iota((CHUNK, CHUNK), 0) == iota((CHUNK, CHUNK), 1)
+    places = tile_places(columns)
     for d in range(blocks):
         at = table_s[chunks + d, 0]
         held = table_s[chunks + d + 1, 0] - at
         named = iota((CHUNK, CHUNK), 0) < held
         count = jnp.where(named, numbers[pl.ds(at, CHUNK), :], 1.0)
         mean = jnp.where(named, sums[pl.ds(at, CHUNK), :] / count, 0.0)
-        pillars[pl.ds(d * CHUNK, CHUNK), :] = mean.astype(BF16)
+        pillars[places(d), :] = mean.astype(BF16)
         counts[d : d + 1, :] = jnp.sum(jnp.where(diagonal, count, 0.0), axis=0, keepdims=True)
 
 
-def pool(points, point_pillar, weight, slots):
+def pool(columns, points, point_pillar, weight, slots):
     total = point_pillar.shape[0]
     chunks, blocks = total // CHUNK, slots // CHUNK
     channels = weight.shape[1]
     rows = chunks + blocks + 8
     vmem = pl.BlockSpec(memory_space=pltpu.VMEM)
     return pl.pallas_call(
-        pool_kernel,
+        functools.partial(pool_kernel, columns),
         out_shape=(
             jax.ShapeDtypeStruct((slots, channels), BF16),
             jax.ShapeDtypeStruct((rows, CHUNK), jnp.int32),
@@ -134,10 +154,6 @@
         spans.append((at, size))
         at += size
     return spans, at
-
-
-def ring_size(columns):
-    return {32: 8, 8: 4, 4: 2}[columns]
 
 
 def ring_order(ring):
@@ -305,20 +321,29 @@
         copy.start()
         started.append(copy)
 
-    def send_pillars(r):
+    groups = {8: [(6, 8), (0, 2), (4, 6), (2, 4)], 4: [(2, 4), (0, 2)], 2: [(0, 2)]}[ring]
+    waited = set()
+
+    def block(o, rel):
+        return pl.ds((o * ring + rel + half_ring - 1) * CHUNK, CHUNK)
+
+    def span(o, group):
+        return pl.ds((o * ring + group[0]) * CHUNK, (group[1] - group[0]) * CHUNK)
+
+    def send_pillars(g):
         for o in range(1, across):
+            rows = span(o, groups[g])
             go(
                 remote(
-                    pillars.at[slot_block(over(o), along(order[r]))],
-                    got_x.at[pl.ds((r * across + o) * CHUNK, CHUNK)],
-                    sem_x.at[0, r, o],
-                    sem_x.at[1, r, o],
+                    pillars.at[rows],
+                    got_x.at[rows],
+                    sem_x.at[0, g, o],
+                    sem_x.at[1, g, o],
                     across_device(o),
                 )
             )
 
-    for r in range(min(3, ring)):
-        send_pillars(r)
+    send_pillars(0)
 
     send_i[...] = jnp.zeros_like(send_i)
     for step in range(ring):
@@ -382,19 +407,8 @@
             axis=0,
         )
 
-    masks = jnp.concatenate([mask_t[...], mask_t[...] * occupied_t[...]], axis=0)
-    masks = masks.astype(F32).astype(BF16)
-    of_row = iota((count, tile_rows), 0) // tile_cols == iota((count, tile_rows), 1)
-    by_column = dot_nt(jnp.where(of_row, 1.0, 0.0).astype(BF16), masks)
-    pairs = (count, 2 * tile_cols)
-    of_column = iota(pairs, 0) % tile_cols == iota(pairs, 1) % tile_cols
-    halves = (2 * tile_cols, channels)
-    same_half = (iota(halves, 0) < tile_cols) == (iota(halves, 1) < channels // 2)
-    mask_own = dot(
-        jnp.where(of_column, by_column, 0.0).astype(BF16),
-        jnp.where(same_half, 1.0, 0.0).astype(BF16),
-    )
-    post(mask_own, send_m, got_m, sem_m)
+    if len(groups) > 1:
+        send_pillars(1)
 
     flat = iota((height * width, channels), 0)
     row = flat // width + gy * tile_rows - HALO
@@ -446,11 +460,15 @@
         )
 
     def placed_for(r):
-        for o in range(1, across):
-            arrival(got_x.at[pl.ds((r * across + o) * CHUNK, CHUNK)], sem_x.at[1, r, o])
-        own = pillars[slot_block(x, along(order[r])), :]
-        rest = got_x[pl.ds((r * across + 1) * CHUNK, fan - CHUNK), :]
-        return dot(place[r], jnp.concatenate([own, rest], axis=0))
+        place_at = order[r] + half_ring - 1
+        for g, group in enumerate(groups):
+            if group[0] <= place_at < group[1] and g not in waited:
+                waited.add(g)
+                for o in range(1, across):
+                    arrival(got_x.at[span(o, group)], sem_x.at[1, g, o])
+        rows = [pillars[block(0, order[r]), :]]
+        rows += [got_x[block(o, order[r]), :] for o in range(1, across)]
+        return dot(place[r], jnp.concatenate(rows, axis=0))
 
     halves = (pl.ds(0, part_rows), pl.ds(part_rows, part_rows))
 
@@ -474,8 +492,6 @@
 
     left = list(range(ring))
     for t in range(half_ring):
-        for r in range(2 * t + 1, min(2 * t + 3, ring)) if t else ():
-            send_pillars(r)
         if t == 0:
             build_place(0)
             summed = placed_for(0)
@@ -494,6 +510,22 @@
                     half = 1 - side if order_half == 0 else side
                     if t > 1 or half == side:
                         grow(t, side, half, half_of(summed[side], half))
+        if t + 2 < len(groups):
+            send_pillars(t + 2)
+        if t == 0:
+            masks = jnp.concatenate([mask_t[...], mask_t[...] * occupied_t[...]], axis=0)
+            masks = masks.astype(F32).astype(BF16)
+            of_row = iota((count, tile_rows), 0) // tile_cols == iota((count, tile_rows), 1)
+            by_column = dot_nt(jnp.where(of_row, 1.0, 0.0).astype(BF16), masks)
+            pairs = (count, 2 * tile_cols)
+            of_column = iota(pairs, 0) % tile_cols == iota(pairs, 1) % tile_cols
+            both = (2 * tile_cols, channels)
+            same_half = (iota(both, 0) < tile_cols) == (iota(both, 1) < channels // 2)
+            mask_own = dot(
+                jnp.where(of_column, by_column, 0.0).astype(BF16),
+                jnp.where(same_half, 1.0, 0.0).astype(BF16),
+            )
+            post(mask_own, send_m, got_m, sem_m)
         for r in left[:2]:
             build_pick(r)
         left = left[2:]
@@ -566,17 +598,22 @@
         )
 
     def hand_out(rel, gradient):
-        r = slot_of[rel]
-        rows = dot(pick[r], gradient).astype(BF16)
-        returned[slot_block(x, along(rel)), :] = rows[:CHUNK]
-        send_r[r] = rows
+        rows = dot(pick[slot_of[rel]], gradient).astype(BF16)
+        returned[block(0, rel), :] = rows[:CHUNK]
         for o in range(1, across):
+            send_r[block(o, rel), :] = rows[o * CHUNK : (o + 1) * CHUNK]
+
+    back_groups = {8: [(2, 5), (5, 6), (0, 2), (6, 8)], 4: [(0, 3), (3, 4)], 2: [(0, 2)]}[ring]
+
+    def send_back(g):
+        for o in range(1, across):
+            rows = span(o, back_groups[g])
             go(
                 remote(
-                    send_r.at[r, pl.ds(o * CHUNK, CHUNK)],
-                    returned.at[slot_block(x, along(rel))],
-                    sem_r.at[0, r, o],
-                    sem_r.at[1, r, o],
+                    send_r.at[rows],
+                    returned.at[rows],
+                    sem_r.at[0, g, o],
+                    sem_r.at[1, g, o],
                     across_device(-o),
                 )
             )
@@ -673,10 +710,12 @@
 
     scale = turned(1.0 / counts[...])
 
+    places = tile_places(n_gx)
+
     def start_merge():
         for d in range(blocks):
-            part = pl.ds(d * CHUNK, CHUNK)
-            merge_a[part, :] = returned[part, :].astype(F32) * scale[:, d : d + 1]
+            block_d = returned[places(d), :].astype(F32)
+            merge_a[pl.ds(d * CHUNK, CHUNK), :] = block_d * scale[:, d : d + 1]
         spare = merge_a.shape[0] - blocks * CHUNK
         for ref in (merge_a, merge_b):
             ref[pl.ds(blocks * CHUNK, spare), :] = jnp.zeros((spare, CHUNK), F32)
@@ -735,7 +774,6 @@
         if t == 1:
             to_levels()
         if t == half_ring:
-            to_pieces(gathered(got_kz, sem_kz))
             hand_out(
                 t,
                 jnp.concatenate(
@@ -745,47 +783,42 @@
         else:
             hand_out(-t, got_g[0, t - 1])
             hand_out(t, got_g[1, t - 1])
+        send_back(t - 1)
+        if t == half_ring:
+            to_pieces(gathered(got_kz, sem_kz))
         share_to = chunks * t // half_ring
         prepare(prepared, share_to)
         prepared = share_to
     to_all(gathered(got_kx, sem_kx), got_ky, sem_ky, y, ring_device)
-    for r, rel in enumerate(order):
+    for g, group in enumerate(back_groups):
         for o in range(1, across):
-            arrival(returned.at[slot_block(over(o), along(rel))], sem_r.at[1, r, o])
+            arrival(returned.at[span(o, group)], sem_r.at[1, g, o])
     start_merge()
     merge(0, min(2, levels_m))
     to_all(take_step(gathered(got_ky, sem_ky)), got_ax, sem_ax, x, across_device)
     merge(min(2, levels_m), levels_m)
     for step in range(1, across):
         arrival(got_ax.at[0], sem_ax.at[1, step])
-    conv_out[gy] = got_ax[...].reshape(across * piece, channels)[:share]
-    mine = conv_out.at[gy]
+    conv_out[z, core] = got_ax[...].reshape(across * piece, channels)[:share]
+    mine = conv_out.at[z, core]
     for step in range(1, levels):
         go(remote(mine, mine, sem_az.at[0, step], sem_az.at[1, step], level_device(step)))
-    go(remote(mine, mine, sem_ac.at[0, 0], sem_ac.at[1, 0], other_core))
     features_in = points.shape[0]
     own_s[...] = jnp.zeros_like(own_s)
     own_s[0:features_in, :] = point_terms()
     own_s[features_in : features_in + 1, :] = head_local
     to_all(own_s[...], got_sy, sem_sy, y, ring_device)
 
-    def relay(begin, end):
-        for step in range(begin, end):
-            held = conv_out.at[lax.rem(z - step + levels, levels) * 2 + core]
-            arrival(held, sem_az.at[1, step])
-            go(remote(held, held, sem_ac.at[0, step], sem_ac.at[1, step], other_core))
-
-    relay(1, min(3, levels))
     to_all(gathered(got_sy, sem_sy), got_sx, sem_sx, x, across_device)
-    relay(min(3, levels), min(6, levels))
+    for step in range(1, levels):
+        arrival(conv_out.at[lax.rem(z - step + levels, levels), core], sem_az.at[1, step])
+    chip = conv_out.at[:, core]
+    go(remote(chip, chip, sem_ac.at[0], sem_ac.at[1], other_core))
     to_all(gathered(got_sx, sem_sx), got_sz, sem_sz, gy, stack_device)
-    relay(min(6, levels), levels)
     small = gathered(got_sz, sem_sz)
     point_out[...] = rms_step(small[:features_in], point_second[...])
     head_out[...] = rms_step(small[features_in : features_in + 1], head_second[...])
-    for step in range(levels):
-        level = lax.rem(z - step + levels, levels)
-        arrival(conv_out.at[level * 2 + 1 - core], sem_ac.at[1, step])
+    arrival(conv_out.at[:, 1 - core], sem_ac.at[1])
     for copy in started:
         copy.wait_send()
 
@@ -812,7 +845,7 @@
     return pl.pallas_call(
         functools.partial(map_kernel, grid),
         out_shape=(
-            jax.ShapeDtypeStruct((n_gy, share, channels), BF16),
+            jax.ShapeDtypeStruct((levels, 2, share, channels), BF16),
             jax.ShapeDtypeStruct(point_weight.shape, F32),
             jax.ShapeDtypeStruct((1, channels), F32),
         ),
@@ -836,7 +869,7 @@
             pltpu.VMEM((2, half_ring, count, channels), BF16),
             pltpu.VMEM((count, channels), BF16),
             pltpu.VMEM((2, half_ring, count, channels), BF16),
-            pltpu.VMEM((ring, across * CHUNK, channels), BF16),
+            pltpu.VMEM((slots, channels), BF16),
             pltpu.VMEM((slots, channels), BF16),
             pltpu.VMEM((levels, 2, share, channels), BF16),
             pltpu.VMEM((levels, share, channels), BF16),
@@ -869,7 +902,7 @@
             pltpu.SemaphoreType.DMA((2, ring)),
             pltpu.SemaphoreType.DMA((2, across)),
             pltpu.SemaphoreType.DMA((2, levels)),
-            pltpu.SemaphoreType.DMA((2, levels)),
+            pltpu.SemaphoreType.DMA((2,)),
             pltpu.SemaphoreType.DMA((2, ring)),
             pltpu.SemaphoreType.DMA((2, across)),
             pltpu.SemaphoreType.DMA((2, n_gy)),
@@ -916,7 +949,7 @@
     slots = recv_cell.shape[0]
     grid = (rows, columns, tile_rows, tile_cols)
 
-    pillars, table, local, counts = pool(points, point_pillar, point_weight, slots)
+    pillars, table, local, counts = pool(columns, points, point_pillar, point_weight, slots)
     conv_step, point_step, head_step = map_step(
         grid,
         pillars,

time: 107 us -> 109 us (1.019)
  Pallas kernels: 103 us -> 105 us
    pallas_call x1, Pallas kernels: 96.4 us -> 98.9 us  [map_step(): pl.pallas_call(functools.partial(map_kernel, grid), out_shape=(jax.ShapeD...]
where the time goes in v5:
time: 109 us
  Pallas kernels  105 us (96%)
  other arithmetic  2.2 us (2%)
  local copies, waits for them, and re-layouts  1.12 us (1%)
    pallas_call x1, Pallas kernels, map_step(): pl.pallas_call(functools.partial(map_kernel, grid), out_shape=(jax.ShapeD...  98.9 us
    pallas_call x1, Pallas kernels, pool(): pl.pallas_call(functools.partial(pool_kernel, columns), out_shape=(jax.Sh...  6.29 us
    reshape x1, other arithmetic, on_device(): conv_step.astype(F32).reshape(conv_second.shape)  2.2 us

profile of v5, /device:TPU:1, one launch (start us, length us, event | category | flops | bytes accessed | tf_op | source)
XLA Modules:
  0.0 109.2 jit_solution(3168684337381694224)
XLA Ops:
  0.6 6.3 %pool.1 = (bf16[4096,128]{1,0:T(8,128)(2,1)}, s32[72,128]{1,0:T(8,128)}, s32[32,128]{1,0:T(8,128)}, f32[32,128]{1,0:T(8,128)}) custom-call(bf16[9,4096]{1,0:T(8,128)(2,1)} %points.3, s32[32,128]{1,0:T(8,128)} %bitcast.15, s32[1,4096]{1,0:T(1,128)} %bitcast.16, bf16[9,128]{1,0:T(8,128)(2,1)} %point_weight.1), custom_call_target="tpu_custom_call" | custom-call | tf_op jit(solution)/shard_map/pool/pallas_call | solution.py:128
  6.9 98.9 %map_step.1 = (bf16[8,2,144,128]{3,2,1,0:T(8,128)(2,1)}, f32[9,128]{1,0:T(8,128)}, f32[1,128]{1,0:T(1,128)}) custom-call(bf16[4096,128]{1,0:T(8,128)(2,1)} %get-tuple-element.10.pillars, s32[32,128]{1,0:T(8,128)} %bitcast.17, s32[16,32]{1,0:T(8,128)} %bitcast.18, s32[16,32]{1,0:T(8,128)} %bitcast.19, bf16[2,1152,128]{2,1,0:T(8,128)(2,1)} %bitcast.14, ...), custom_call_target="tpu_custom_call" | custom-call | tf_op jit(solution)/shard_map/map_step/pallas_call | solution.py:845
  105.9 0.0 copy-start
  105.9 0.0 copy-start.1
  105.9 2.2 %convert.1 = f32[2,9,128,128]{3,2,1,0:T(8,128)} convert(bf16[2,9,128,128]{3,2,1,0:T(8,128)(2,1)} %bitcast.13) | non-fusion elementwise | flops 294912 | bytes 1769472 | tf_op jit(solution)/shard_map/reshape | solution.py:970
  108.1 0.0 copy-done
  108.1 0.6 copy.16
  108.7 0.0 copy-done.1
  108.7 0.5 copy.17
Async XLA Ops:
  105.9 2.2 %copy-start = (f32[9,128]{1,0:T(8,128)S(1)}, f32[9,128]{1,0:T(8,128)}, u32[]{:S(2)}) copy-start(f32[9,128]{1,0:T(8,128)} %get-tuple-element.21) | copy-start | bytes 13828
  105.9 2.8 %copy-start.1 = (f32[1,128]{1,0:T(1,128)S(1)}, f32[1,128]{1,0:T(1,128)}, u32[]{:S(2)}) copy-start(f32[1,128]{1,0:T(1,128)} %get-tuple-element.16) | copy-start | bytes 1540

commit v6 on v2

--- a/solution.py
+++ b/solution.py
@@ -597,6 +597,11 @@
             )
         )
 
+    def kernel_gradient(ref, lead, gradient):
+        by_output = dot_tn(gradient, windows(ref, lead, tile_rows))
+        taps = [by_output[:, k * channels : (k + 1) * channels].T for k in range(9)]
+        return jnp.concatenate(taps, axis=0)
+
     def to_levels():
         for layer in (0, 1):
             arrival(core_k.at[pl.ds(layer * parts, parts)], sem_c.at[1, layer])
@@ -714,9 +719,9 @@
         for side in (0, 1):
             pass_on(1, side, side if order_half == 0 else 1 - side)
     own1 = (cut(grad1, 1, tile_rows) * own_column).astype(BF16)
-    halve(0, dot_tn(windows(v0, 3, tile_rows), own1))
+    halve(0, kernel_gradient(v0, 3, own1))
     own2 = (cut(grad2, 2, tile_rows) * own_column).astype(BF16)
-    halve(1, dot_tn(windows(v1, 2, tile_rows), own2))
+    halve(1, kernel_gradient(v1, 2, own2))
     hand_out(0, own_g[...])
     head_terms = cut(logit_grad * hidden2.astype(F32), 2, tile_rows) * own_column
     head_local = jnp.sum(head_terms, axis=0, keepdims=True)

time: 107 us -> 107 us (level)
  no operation moved by 1% of the time
where the time goes in v6:
time: 107 us
  Pallas kernels  103 us (96%)
  other arithmetic  2.2 us (2%)
  local copies, waits for them, and re-layouts  1.12 us (1%)
    pallas_call x1, Pallas kernels, map_step(): pl.pallas_call(functools.partial(map_kernel, grid), out_shape=(jax.ShapeD...  96.3 us
    pallas_call x1, Pallas kernels, pool(): pl.pallas_call(pool_kernel, out_shape=(jax.ShapeDtypeStruct((slots, chann...  6.28 us
    reshape x1, other arithmetic, on_device(): conv_step.astype(F32).reshape(conv_second.shape)  2.2 us

profile of v6, /device:TPU:1, one launch (start us, length us, event | category | flops | bytes accessed | tf_op | source)
XLA Modules:
  0.0 106.6 jit_solution(6705184577937502655)
XLA Ops:
  0.6 6.3 %pool.1 = (bf16[4096,128]{1,0:T(8,128)(2,1)}, s32[72,128]{1,0:T(8,128)}, s32[32,128]{1,0:T(8,128)}, f32[32,128]{1,0:T(8,128)}) custom-call(bf16[9,4096]{1,0:T(8,128)(2,1)} %points.3, s32[32,128]{1,0:T(8,128)} %bitcast.15, s32[1,4096]{1,0:T(1,128)} %bitcast.16, bf16[9,128]{1,0:T(8,128)(2,1)} %point_weight.1), custom_call_target="tpu_custom_call" | custom-call | tf_op jit(solution)/shard_map/pool/pallas_call | solution.py:108
  6.9 96.3 %map_step.1 = (bf16[16,144,128]{2,1,0:T(8,128)(2,1)}, f32[9,128]{1,0:T(8,128)}, f32[1,128]{1,0:T(1,128)}) custom-call(bf16[4096,128]{1,0:T(8,128)(2,1)} %get-tuple-element.10.pillars, s32[32,128]{1,0:T(8,128)} %bitcast.17, s32[16,32]{1,0:T(8,128)} %bitcast.18, s32[16,32]{1,0:T(8,128)} %bitcast.19, bf16[2,1152,128]{2,1,0:T(8,128)(2,1)} %bitcast.14, ...), custom_call_target="tpu_custom_call" | custom-call | tf_op jit(solution)/shard_map/map_step/pallas_call | solution.py:817
  103.2 0.0 copy-start
  103.2 0.0 copy-start.1
  103.3 2.2 %convert.1 = f32[2,9,128,128]{3,2,1,0:T(8,128)} convert(bf16[2,9,128,128]{3,2,1,0:T(8,128)(2,1)} %bitcast.13) | non-fusion elementwise | flops 294912 | bytes 1769472 | tf_op jit(solution)/shard_map/reshape | solution.py:942
  105.5 0.0 copy-done
  105.5 0.6 copy.16
  106.1 0.0 copy-done.1
  106.1 0.5 copy.17
Async XLA Ops:
  103.2 2.2 %copy-start = (f32[9,128]{1,0:T(8,128)S(1)}, f32[9,128]{1,0:T(8,128)}, u32[]{:S(2)}) copy-start(f32[9,128]{1,0:T(8,128)} %get-tuple-element.21) | copy-start | bytes 13828
  103.2 2.8 %copy-start.1 = (f32[1,128]{1,0:T(1,128)S(1)}, f32[1,128]{1,0:T(1,128)}, u32[]{:S(2)}) copy-start(f32[1,128]{1,0:T(1,128)} %get-tuple-element.16) | copy-start | bytes 1540
